TPU v7x, 256 devices: a whole 4x4x8 slice. The times are simulated.
256 devices in a mesh: dp: 16 (over y, x_hi, core), tensor: 16 (over x_lo, z).
Axes of the slice: x: 4 (x_hi: 2, x_lo: 2; x = x_hi * 2 + x_lo), y: 4, z: 8, core: 2. Of those that a mesh axis runs over, the one named last changes fastest.
Arguments:
- tokens: bfloat16 [8192, 2304], P('dp', 'tensor'), may hold values from -6 to 6
- cotangent: bfloat16 [8192, 2304], P('dp', 'tensor'), may hold values from -6 to 6
- prune_mask: int32 [18, 9216], P(None, 'tensor'), may hold values 0 or 1
- w_gate_up: bfloat16 [2, 2304, 9216], P(None, 'dp', 'tensor'), may hold values from -0.1875 to 0.1875
- w_down: bfloat16 [9216, 2304], P('tensor', 'dp'), may hold values from -0.0625 to 0.0625
- m_gate_up: float32 [2, 2304, 9216], P(None, 'dp', 'tensor'), may hold values from -2 to 2
- v_gate_up: float32 [2, 2304, 9216], P(None, 'dp', 'tensor'), may hold values from 0.01 to 0.3
- m_down: float32 [9216, 2304], P('tensor', 'dp'), may hold values from -2 to 2
- v_down: float32 [9216, 2304], P('tensor', 'dp'), may hold values from 0.01 to 0.3
Outputs:
- input_grad: bfloat16 [8192, 2304], P('dp', 'tensor')
- m_gate_up_new: float32 [2, 2304, 9216], P(None, 'dp', 'tensor')
- v_gate_up_new: float32 [2, 2304, 9216], P(None, 'dp', 'tensor')
- step_gate_up: float32 [2, 2304, 9216], P(None, 'dp', 'tensor')
- m_down_new: float32 [9216, 2304], P('tensor', 'dp')
- v_down_new: float32 [9216, 2304], P('tensor', 'dp')
- step_down: float32 [9216, 2304], P('tensor', 'dp')
All inputs are finite; a program needn't handle non-finite values. No bound on the sum of `prune_mask` on one device may be relied on, other than what follows from the above.
Results may differ from a plain program's by a relative error of at most 0.005.
Values may be sent and summed in bfloat16 or wider, within the bound.
A program may use at most 128 MiB of HBM per device.

v0:
```python
import jax
import jax.numpy as jnp
from jax import lax
from jax.sharding import PartitionSpec as P


def adam_moments(first, second, grad):
    first_new = 0.9 * first + 0.1 * grad
    second_new = 0.95 * second + 0.05 * grad * grad
    return (first_new, second_new, first_new / (jnp.sqrt(second_new) + 1e-08))


def on_device(
    tokens, cotangent, prune_mask, w_gate_up, w_down, m_gate_up, v_gate_up, m_down, v_down
):
    full_gate_up, full_down = (
        lax.all_gather(w_gate_up, "dp", axis=1, tiled=True),
        lax.all_gather(w_down, "dp", axis=1, tiled=True),
    )
    row_count = full_gate_up.shape[1]
    hidden_units = full_gate_up.shape[2]
    blocks = prune_mask.shape[0]
    keep = prune_mask.astype(jnp.bfloat16)
    keep_rows = jnp.broadcast_to(
        keep[:, None, :], (blocks, row_count // blocks, hidden_units)
    ).reshape(row_count, hidden_units)
    eff_gate_up = full_gate_up * keep_rows[None]
    eff_down = full_down * keep_rows.T
    features, cotangents = (
        lax.all_gather(tokens, "tensor", axis=1, tiled=True),
        lax.all_gather(cotangent, "tensor", axis=1, tiled=True),
    )
    both_values = jnp.einsum(
        "td,kdf->ktf", features, eff_gate_up, preferred_element_type=jnp.float32
    )
    gate_value = both_values[0]
    up_value = both_values[1]
    sigmoid_gate = jax.nn.sigmoid(gate_value)
    silu_gate = gate_value * sigmoid_gate
    hidden = (silu_gate * up_value).astype(jnp.bfloat16)
    hidden_grad = jnp.einsum("td,fd->tf", cotangents, eff_down, preferred_element_type=jnp.float32)
    silu_slope = sigmoid_gate * (1.0 + gate_value * (1.0 - sigmoid_gate))
    gate_grad = (hidden_grad * up_value * silu_slope).astype(jnp.bfloat16)
    up_grad = (hidden_grad * silu_gate).astype(jnp.bfloat16)
    both_grads = jnp.stack([gate_grad, up_grad])
    partial_input = jnp.einsum(
        "ktf,kdf->td", both_grads, eff_gate_up, preferred_element_type=jnp.float32
    )
    input_grad = lax.psum_scatter(partial_input, "tensor", scatter_dimension=1, tiled=True).astype(
        jnp.bfloat16
    )
    local_gate_up = jnp.einsum(
        "td,ktf->kdf", features, both_grads, preferred_element_type=jnp.float32
    )
    local_down = jnp.einsum("tf,td->fd", hidden, cotangents, preferred_element_type=jnp.float32)
    grad_gate_up, grad_down = (
        lax.psum_scatter(local_gate_up, "dp", scatter_dimension=1, tiled=True),
        lax.psum_scatter(local_down, "dp", scatter_dimension=1, tiled=True),
    )
    shard_rows = w_gate_up.shape[1]
    grad_scale = jnp.float32(tokens.shape[0] * lax.axis_size("dp")) ** (-0.5)
    own_keep = lax.dynamic_slice_in_dim(
        keep_rows, lax.axis_index("dp") * shard_rows, shard_rows, 0
    ).astype(jnp.float32)
    grad_gate_up = grad_gate_up * grad_scale * own_keep[None]
    grad_down = grad_down * grad_scale * own_keep.T
    m_gate_up_new, v_gate_up_new, step_gate_up = adam_moments(m_gate_up, v_gate_up, grad_gate_up)
    m_down_new, v_down_new, step_down = adam_moments(m_down, v_down, grad_down)
    return (
        input_grad,
        m_gate_up_new,
        v_gate_up_new,
        step_gate_up,
        m_down_new,
        v_down_new,
        step_down,
    )


def solution(mesh):
    return jax.shard_map(
        on_device,
        mesh=mesh,
        in_specs=(
            P("dp", "tensor"),
            P("dp", "tensor"),
            P(None, "tensor"),
            P(None, "dp", "tensor"),
            P("tensor", "dp"),
            P(None, "dp", "tensor"),
            P(None, "dp", "tensor"),
            P("tensor", "dp"),
            P("tensor", "dp"),
        ),
        out_specs=(
            P("dp", "tensor"),
            P(None, "dp", "tensor"),
            P(None, "dp", "tensor"),
            P(None, "dp", "tensor"),
            P("tensor", "dp"),
            P("tensor", "dp"),
            P("tensor", "dp"),
        ),
        check_vma=False,
    )
```

profile of v0, /device:TPU:2, one launch (start us, length us, event | category | flops | bytes accessed | tf_op | source)
XLA Modules:
  0.0 740.9 jit_solution(9101052172775983254)
XLA Ops:
  7.2 0.0 all-gather.9.cloned.1.call-start
  7.2 2.0 copy.36
  9.2 0.0 all-gather.9.cloned.1.call-update
  9.2 0.0 all-gather.11.cloned.1.call-start
  9.3 0.7 all-gather.11.cloned.1.call-update
  10.0 0.0 all-gather.7.cloned.1.call-start
  10.0 0.7 all-gather.7.cloned.1.call-update
  10.7 0.0 all-gather.5.cloned.1.call-start
  10.8 0.5 all-gather.5.cloned.1.call-update
  11.3 0.0 reduce-scatter.5.cloned.1.call-start
  11.4 0.8 convert_element_type.18
  12.2 0.2 broadcast_in_dim.2
  12.4 3.5 copy.37
  15.9 64.9 %all-gather.9.cloned.1.call-done = bf16[2,2304,576]{2,0,1:T(2,128)(2,1)} async-done(((bf16[2,144,576]{2,0,1:T(2,128)(2,1)}), bf16[2,2304,576]{2,0,1:T(2,128)(2,1)}) %all-gather.9.cloned.1.call-update) | async-done | bytes 5308432 | tf_op jit(solution)/shard_map/all_gather | solution.py:17
  80.9 16.6 %copy.38 = bf16[2,2304,576]{1,2,0:T(8,128)(2,1)} copy(bf16[2,2304,576]{2,0,1:T(2,128)(2,1)} %all-gather.9.cloned.1.call-done) | data formatting | bytes 10616832 | tf_op jit(solution)/shard_map/all_gather | solution.py:17
  97.5 55.3 %all-gather.11.cloned.1.call-done = bf16[512,2304]{0,1:T(8,128)(2,1)} async-done(((bf16[512,144]{0,1:T(8,128)(2,1)}), bf16[512,2304]{0,1:T(8,128)(2,1)}) %all-gather.11.cloned.1.call-update) | async-done | bytes 2359312 | tf_op jit(solution)/shard_map/all_gather | solution.py:30
  152.8 8.3 %fusion.7 = f32[2,512,576]{1,2,0:T(8,128)} fusion(bf16[512,2304]{0,1:T(8,128)(2,1)} %all-gather.11.cloned.1.call-done, bf16[2,2304,576]{1,2,0:T(8,128)(2,1)} %copy.38, bf16[2304,576]{0,1:T(8,128)(2,1)} %copy.37), kind=kOutput, calls=%fused_computation.10 | convolution fusion | flops 2720563200 | bytes 12681216 | tf_op jit(solution)/shard_map/td,kdf->ktf/dot_general | solution.py:33
  161.1 63.3 %all-gather.7.cloned.1.call-done = bf16[512,2304]{0,1:T(8,128)(2,1)} async-done(((bf16[512,144]{0,1:T(8,128)(2,1)}), bf16[512,2304]{0,1:T(8,128)(2,1)}) %all-gather.7.cloned.1.call-update) | async-done | bytes 2359312 | tf_op jit(solution)/shard_map/all_gather | solution.py:31
  224.4 7.0 fusion.15
  231.4 0.0 reduce-scatter.5.cloned.1.call-update
  231.4 0.0 reduce-scatter.3.cloned.1.call-start
  231.5 48.1 %all-gather.5.cloned.1.call-done = bf16[576,2304]{0,1:T(8,128)(2,1)} async-done(((bf16[576,144]{0,1:T(8,128)(2,1)}), bf16[576,2304]{0,1:T(8,128)(2,1)}) %all-gather.5.cloned.1.call-update) | async-done | bytes 2654224 | tf_op jit(solution)/shard_map/all_gather | solution.py:18
  279.6 2.3 bitcast_multiply_fusion
  281.9 0.0 slice-start.1
  281.9 0.0 copy-start
  281.9 4.4 fusion.16
  286.3 0.0 copy-start.4
  286.3 0.8 copy-done.4
  287.1 0.0 slice-done
  287.1 0.0 slice-done.1
  287.1 0.0 copy-done
  287.1 4.9 convolution_bitcast_fusion.1
  292.0 0.0 reduce-scatter.3.cloned.1.call-update
  292.1 0.2 all-reduce.3.cloned.1.call-start
  292.3 9.2 %convolution_bitcast_fusion = f32[2,2304,576]{1,2,0:T(8,128)} fusion(bf16[512,2304]{0,1:T(8,128)(2,1)} %all-gather.11.cloned.1.call-done, bf16[1,512,576]{1,2,0:T(8,128)(2,1)} %copy-done.4, bf16[1,512,576]{1,2,0:T(8,128)(2,1)S(1)} %get-tuple-element.27), kind=kOutput, calls=%fused_computation | convolution fusion | flops 2718498816 | bytes 14155776 | tf_op jit(solution)/shard_map/td,ktf->kdf/dot_general | solution.py:52
  301.5 19.4 %copy.39 = f32[2,2304,576]{2,0,1:T(2,128)} copy(f32[2,2304,576]{1,2,0:T(8,128)} %convolution_bitcast_fusion) | data formatting | bytes 21233664 | tf_op jit(solution)/shard_map/td,ktf->kdf/transpose | solution.py:52
  320.9 0.0 all-reduce.3.cloned.1.call-update
  320.9 0.6 copy-done.3
  321.6 0.6 dynamic-slice
  322.9 55.4 %reduce-scatter.5.cloned.1.call-done = f32[576,144]{0,1:T(8,128)} async-done(((f32[576,2304]{0,1:T(8,128)}), f32[576,144]{0,1:T(8,128)}) %reduce-scatter.5.cloned.1.call-update) | async-done | bytes 331792 | tf_op jit(solution)/shard_map/reduce_scatter | solution.py:58
  378.3 2.3 add_divide_fusion.2
  380.6 81.2 %reduce-scatter.3.cloned.1.call-done = f32[512,144]{0,1:T(8,128)} async-done(((f32[512,2304]{0,1:T(8,128)}), f32[512,144]{0,1:T(8,128)}) %reduce-scatter.3.cloned.1.call-update) | async-done | bytes 294928 | tf_op jit(solution)/shard_map/reduce_scatter | solution.py:49
  461.8 1.6 convert_element_type.21
  463.5 267.6 %all-reduce.3.cloned.1.call-done = f32[2,2304,576]{2,0,1:T(2,128)} async-done(((f32[2,2304,576]{2,0,1:T(2,128)}), f32[2,2304,576]{2,0,1:T(2,128)}) %all-reduce.3.cloned.1.call-update) | async-done | bytes 10616848
  731.1 1.4 constant_dynamic-slice_fusion
  732.4 0.0 copy-done.1
  732.4 0.0 copy-done.2
  732.5 1.6 add_divide_fusion.1
  (6 shorter events, 0.0 us)
Async XLA Ops:
  7.2 73.7 %all-gather.9.cloned.1.call-start = ((), (), s32[]{:S(2)}) async-start(), calls=%async_computation.4 | async-start | bytes 6266880 | tf_op jit(solution)/shard_map/all_gather | solution.py:17
  9.2 143.6 %all-gather.11.cloned.1.call-start = ((), (), s32[]{:S(2)}) async-start(), calls=%async_computation.5 | async-start | bytes 2506752 | tf_op jit(solution)/shard_map/all_gather | solution.py:30
  10.0 214.4 %all-gather.7.cloned.1.call-start = ((), (), s32[]{:S(2)}) async-start(), calls=%async_computation.3 | async-start | bytes 2506752 | tf_op jit(solution)/shard_map/all_gather | solution.py:31
  10.7 268.9 %all-gather.5.cloned.1.call-start = ((), (), s32[]{:S(2)}) async-start(), calls=%async_computation.2 | async-start | bytes 3133440 | tf_op jit(solution)/shard_map/all_gather | solution.py:18
  11.3 367.0 %reduce-scatter.5.cloned.1.call-start = ((), (), s32[]{:S(2)}) async-start(), calls=%async_computation.7 | async-start | bytes 6266880 | tf_op jit(solution)/shard_map/reduce_scatter | solution.py:58
  231.4 230.4 %reduce-scatter.3.cloned.1.call-start = ((), (), s32[]{:S(2)}) async-start(), calls=%async_computation.6 | async-start | bytes 5013504 | tf_op jit(solution)/shard_map/reduce_scatter | solution.py:49
  279.6 7.5 %slice-start = ((s8[5308416]{0:T(1024)(128)(4,1)}), s8[4194304]{0:T(1024)(128)(4,1)S(1)}, s32[]{:S(2)}) async-start(s8[5308416]{0:T(1024)(128)(4,1)} %bitcast.64), calls=%async_computation.9 | async-start | bytes 8388608
  281.9 5.3 slice-start.1
  281.9 5.2 copy-start
  286.3 0.8 copy-start.4
  292.1 439.0 %all-reduce.3.cloned.1.call-start = ((), (), s32[]{:S(2)}) async-start(), calls=%async_computation.8 | async-start | bytes 23592960
  320.9 0.7 copy-start.3
  380.6 351.8 %copy-start.1 = (f32[2,144,576]{2,1,0:T(8,128)S(1)}, f32[2,144,576]{2,1,0:T(8,128)}, u32[]{:S(2)}) copy-start(f32[2,144,576]{2,1,0:T(8,128)} %param.15) | copy-start | bytes 1990660
  380.6 351.8 %copy-start.2 = (f32[2,144,576]{2,1,0:T(8,128)S(1)}, f32[2,144,576]{2,1,0:T(8,128)}, u32[]{:S(2)}) copy-start(f32[2,144,576]{2,1,0:T(8,128)} %param.14) | copy-start | bytes 1990660
Sparse Core Ops, SparseCore 0:
  11.3 69.4 all-gather.8
  82.7 70.1 all-gather.10
  154.6 69.6 all-gather.6
  226.9 52.6 all-gather.4
  283.9 94.3 reduce-scatter.4
  380.9 80.8 reduce-scatter.2
  464.7 266.3 all-reduce.2
where the time goes:
time: 743 us; the launch traced here: 741 us
  waiting for transfers between devices  638 us (86%)
  local copies, waits for them, and re-layouts  45.2 us (6%)
  matrix products  33.8 us (5%)
  between operations  14.9 us (2%)
  other arithmetic  8.67 us (1%)
    unnamed x8, waiting for transfers between devices  270 us
    reduce_scatter x1, waiting for transfers between devices, on_device(): lax.psum_scatter(partial_input, 'tensor', scatter_dimension=1, tiled=True)  81.2 us
    all_gather x1, waiting for transfers between devices, on_device(): lax.all_gather(w_gate_up, 'dp', axis=1, tiled=True)  64.9 us
    all_gather x1, waiting for transfers between devices, on_device(): lax.all_gather(cotangent, 'tensor', axis=1, tiled=True)  63.3 us
    reduce_scatter x1, waiting for transfers between devices, on_device(): lax.psum_scatter(local_down, 'dp', scatter_dimension=1, tiled=True)  55.4 us
    all_gather x1, waiting for transfers between devices, on_device(): lax.all_gather(tokens, 'tensor', axis=1, tiled=True)  55.3 us
    all_gather x1, waiting for transfers between devices, on_device(): lax.all_gather(w_down, 'dp', axis=1, tiled=True)  48.1 us
    transpose x1, local copies, waits for them, and re-layouts, on_device(): jnp.einsum('td,ktf->kdf', features, both_grads, preferred_element_type=jn...  19.4 us
  transfers between devices with their start and end apart: 7, of which 7 were waited for; matrix products, arithmetic and copies ran while one was open for 11% of the time, Pallas kernels for 0%

commit v1 on v0

v1 whole, which is shorter than its diff:
```python
import functools
import jax
import jax.numpy as jnp
from jax import lax
from jax.experimental import pallas as pl
from jax.experimental.pallas import tpu as pltpu
from jax.sharding import PartitionSpec as P

BF = jnp.bfloat16
F32 = jnp.float32
MESH = pl.DeviceIdType.MESH

D = 2304
S = 144
T = 512
F = 576
MAIN = 512
GU = 1152
PK = 1792
CUTS = (((0, 80), (80, 64)), ((80, 64), (0, 80)))
COPIES = 80


def dot(a, b, ca, cb):
    return lax.dot_general(a, b, (((ca,), (cb,)), ((), ())), preferred_element_type=F32)


def rows(start, count, step=16):
    return pl.ds(pl.multiple_of(start, step), count)


def keep_of(mask_ref, dp):
    block = dp + dp // 8
    first = 128 - 16 * (dp % 8)
    row = lax.broadcasted_iota(jnp.int32, (S, F), 0)
    return jnp.where(row < first, mask_ref[pl.ds(block, 1), :], mask_ref[pl.ds(block + 1, 1), :])


def pack(ref, at, keep, gate, up, down):
    gate, up, down = (jnp.where(keep != 0, w.astype(F32), 0.0) for w in (gate, up, down))
    ref[at, 0:MAIN] = gate[:, :MAIN].astype(BF)
    ref[at, MAIN : 2 * MAIN] = up[:, :MAIN].astype(BF)
    ref[at, 2 * MAIN : GU] = jnp.concatenate([gate[:, MAIN:], up[:, MAIN:]], 1).astype(BF)
    ref[at, GU : GU + MAIN] = down[:, :MAIN].astype(BF)
    rest = down[:, MAIN:]
    ref[at, GU + MAIN : PK] = jnp.concatenate([rest, jnp.zeros_like(rest)], 1).astype(BF)


def add_rows(dst, to, n, *srcs):
    @pl.loop(0, n // 16)
    def _(i):
        at = rows(to + i * 16, 16)
        total = dst[at, :].astype(F32)
        for src, start in srcs:
            total += src[rows(start + i * 16, 16), :].astype(F32)
        dst[at, :] = total.astype(dst.dtype)


def grads_of(gate, up, hidden_grad):
    sig = jax.nn.sigmoid(gate)
    silu = gate * sig
    gate_grad = hidden_grad * up * (sig * (1.0 + gate * (1.0 - sig)))
    return gate_grad, hidden_grad * silu, silu * up


def hidden_pass(a, w, g, h):
    @pl.loop(0, 2)
    def _(m):
        tok = rows(m * 256, 256, 256)
        cot = rows(T + m * 256, 256, 256)

        @pl.loop(0, 2)
        def _(j):
            lo = rows(j * 256, 256, 256)
            hi = rows(MAIN + j * 256, 256, 256)
            gate = dot(a[:, tok], w[:, lo], 0, 0)
            up = dot(a[:, tok], w[:, hi], 0, 0)
            hg = dot(a[:, cot], w[:, rows(GU + j * 256, 256, 128)], 0, 0)
            gate_grad, up_grad, hidden = grads_of(gate, up, hg)
            g[tok, lo] = gate_grad.astype(BF)
            g[tok, hi] = up_grad.astype(BF)
            h[tok, lo] = hidden.astype(BF)

        both = dot(a[:, tok], w[:, 2 * MAIN : GU], 0, 0)
        hg = dot(a[:, cot], w[:, GU + MAIN : PK], 0, 0)
        gate_grad, up_grad, hidden = grads_of(both, pltpu.roll(both, 64, 1), hg)
        low = lax.broadcasted_iota(jnp.int32, (256, 128), 1) < 64
        g[tok, 2 * MAIN : GU] = jnp.where(low, gate_grad, pltpu.roll(up_grad, 64, 1)).astype(BF)
        h[tok, MAIN:640] = jnp.where(low, hidden, 0.0).astype(BF)


def body(tok_ref, cot_ref, mask_ref, wgu_ref, wd_ref, grad_ref, ig_ref,
         a, w, p, g, h, ig, sib, ya, yb, xb, za, zh, xl, send_sem, recv_sem):
    dp, tensor = lax.axis_index("dp"), lax.axis_index("tensor")
    y, hi, c = dp // 4, (dp // 2) % 2, dp % 2
    lo, z = tensor // 8, tensor % 8
    hk = (hi, 1 - hi)
    lk = (lo, 1 - lo)

    def dp_at(dy, k, flip=0):
        return (((y + dy) % 4) * 2 + hk[k]) * 2 + (1 - c if flip else c)

    def t_at(dz, k):
        return lk[k] * 8 + (z + dz) % 8

    up_y, down_y = (dp_at(1, 0), tensor), (dp_at(3, 0), tensor)
    up_z, down_z = (dp, t_at(1, 0)), (dp, t_at(7, 0))
    other_h, other_l, sibling = (dp_at(0, 1), tensor), (dp, t_at(0, 1)), (dp_at(0, 0, 1), tensor)
    ydev, zdev = (up_y, down_y), (up_z, down_z)

    barrier = pltpu.get_barrier_semaphore()
    partners = (up_y, down_y, up_z, down_z, other_h, other_l, sibling)
    for dev in partners:
        pl.semaphore_signal(barrier, inc=1, device_id=dev, device_id_type=MESH)

    sent = []

    def send(src, dst, dev):
        n = len(sent)
        copy = pltpu.make_async_remote_copy(
            src, dst, send_sem.at[n], recv_sem.at[n], device_id=dev, device_id_type=MESH
        )
        copy.start()
        sent.append(copy)
        return copy

    def got(*copies):
        for copy in copies:
            copy.wait_recv()

    def same(ref, start, count, dev):
        part = ref.at[rows(start, count)]
        return send(part, part, dev)

    def wrow(dy, k, flip=0):
        return dp_at(dy, k, flip) * S

    def arow(dz, k):
        return t_at(dz, k) * S

    own_a = rows(arow(0, 0), S)
    a[own_a, 0:T] = tok_ref[...].T
    a[own_a, T : 2 * T] = cot_ref[...].T
    keep = keep_of(mask_ref, dp)
    pack(w, rows(wrow(0, 0), S), keep, wgu_ref[0], wgu_ref[1], wd_ref[...].T)
    pl.semaphore_wait(barrier, len(partners))

    a_x = same(a, arow(0, 0), S, other_l)
    a0 = [same(a, arow(0, 0), S, d) for d in zdev]
    w0 = [same(w, wrow(0, 0), S, d) for d in ydev]
    w_x = same(w, wrow(0, 0), S, other_h)
    w_c = [same(w, wrow(0, 0), S, sibling)]

    def w_next(k, first):
        halves = []
        for way, (copy, dy) in enumerate(zip(first, (3, 1))):
            got(copy)
            start, count = CUTS[k][way]
            halves.append(same(w, wrow(dy, k) + start, count, ydev[way]))
            w_c.append(same(w, wrow(dy, k), S, sibling))
        return halves

    def w_last(k, halves):
        got(*halves)
        w_c.append(same(w, wrow(2, k), S, sibling))

    def a_next(k, copies, d):
        out = []
        for way, (copy, dz) in enumerate(zip(copies, (8 - d, d))):
            got(copy)
            start, count = CUTS[k][way] if d == 3 else (0, S)
            out.append(same(a, arow(dz, k) + start, count, zdev[way]))
        return out

    a1 = a_next(0, a0, 1)
    got(a_x)
    b0 = [same(a, arow(0, 1), S, d) for d in zdev]
    w1 = w_next(0, w0)
    got(w_x)
    v0 = [same(w, wrow(0, 1), S, d) for d in ydev]
    w_c.append(same(w, wrow(0, 1), S, sibling))
    a2 = a_next(0, a1, 2)
    b1 = a_next(1, b0, 1)
    w_last(0, w1)
    a3 = a_next(0, a2, 3)
    a_l = [same(a, arow(dz, 0), S, other_l) for dz in (5, 3)]
    v1 = w_next(1, v0)
    got(*a3)
    a_l.append(same(a, arow(4, 0), S, other_l))
    got(*b1)
    w_last(1, v1)
    got(*a_l, *w_c)

    hidden_pass(a, w, g, h)

    def weight_grads(dy):
        at = rows(((y + dy) % 4) * 4 * S, 4 * S)
        p[at, 0:GU] = dot(a[at, 0:T], g[...], 1, 0).astype(BF)
        p[at, GU:PK] = dot(a[at, T : 2 * T], h[...], 1, 0).astype(BF)
        out = {}
        for k in (1, 0):
            to = sib.at[rows((dp_at(dy, k) // 2) * S, S)]
            out[k] = send(p.at[rows(wrow(dy, k, 1), S)], to, sibling)
        return out

    def with_sibling(dy, k, copies):
        got(copies[k])
        add_rows(p, wrow(dy, k), S, (sib, (dp_at(dy, k) // 2) * S))

    def ya_row(k, way):
        return (k * 2 + way) * 80

    def yb_row(k, way):
        return (k * 2 + way) * S

    def y_far(k):
        out = []
        for way in (0, 1):
            start, count = CUTS[k][way]
            src = p.at[rows(wrow(2, k) + start, count)]
            out.append(send(src, ya.at[rows(ya_row(k, way), count)], ydev[way]))
        return out

    def y_near(k, way, part):
        start, count = CUTS[k][part]
        src = p.at[rows(wrow((1, 3)[way], k) + start, count)]
        return send(src, yb.at[rows(yb_row(k, way) + start, count)], ydev[way])

    def y_pass(k, far):
        out = []
        for way in (0, 1):
            got(far[way])
            start, count = CUTS[k][way]
            add_rows(p, wrow((1, 3)[way], k) + start, count, (ya, ya_row(k, way)))
            out.append(y_near(k, way, way))
        return out

    s2 = weight_grads(2)
    s1 = weight_grads(1)
    with_sibling(2, 1, s2)
    far1 = y_far(1)
    s3 = weight_grads(3)
    with_sibling(1, 1, s1)
    near1 = [y_near(1, 0, 1)]
    with_sibling(3, 1, s3)
    near1.append(y_near(1, 1, 0))
    with_sibling(2, 0, s2)
    far0 = y_far(0)
    s0 = weight_grads(0)

    @pl.loop(0, 2)
    def _(i):
        at = rows(i * 1152, 1152)
        ig[at, :] = dot(w[at, 0:GU], g[...], 1, 1).astype(BF)

    def za_row(k, way, step):
        return ((k * 2 + way) * 3 + step) * S

    def z_far(k):
        out = []
        for way in (0, 1):
            start, count = CUTS[k][way]
            src = ig.at[rows(arow(4, k) + start, count)]
            out.append(send(src, zh.at[rows((k * 2 + way) * 80, count)], zdev[way]))
        return out

    def z_pass(k, copies, d):
        out = []
        for way, dz in enumerate((d, 8 - d)):
            got(copies[way])
            if d == 3:
                start, count = CUTS[k][way]
                add_rows(ig, arow(dz, k) + start, count, (zh, (k * 2 + way) * 80))
            else:
                add_rows(ig, arow(dz, k), S, (za, za_row(k, way, 2 - d)))
            src = ig.at[rows(arow(dz, k), S)]
            out.append(send(src, za.at[rows(za_row(k, way, 3 - d), S)], zdev[way]))
        return out

    zc = {k: z_far(k) for k in (1, 0)}
    near1 += y_pass(1, far1)
    zc = {k: z_pass(k, zc[k], 3) for k in (1, 0)}
    with_sibling(1, 0, s1)
    near0 = [y_near(0, 0, 1)]
    with_sibling(3, 0, s3)
    near0.append(y_near(0, 1, 0))
    zc = {k: z_pass(k, zc[k], 2) for k in (1, 0)}
    near0 += y_pass(0, far0)
    zc = {k: z_pass(k, zc[k], 1) for k in (1, 0)}
    got(*zc[1])
    add_rows(ig, arow(0, 1), S, (za, za_row(1, 0, 2)), (za, za_row(1, 1, 2)))
    z_x = send(ig.at[rows(arow(0, 1), S)], xl, other_l)
    got(s0[1], *near1)
    own = (dp_at(0, 1) // 2) * S
    add_rows(p, wrow(0, 1), S, (sib, own), (yb, yb_row(1, 0)), (yb, yb_row(1, 1)))
    y_x = send(p.at[rows(wrow(0, 1), S)], xb, other_h)

    got(*zc[0], z_x)
    total = ig[rows(arow(0, 0), S), :].astype(F32) + xl[...].astype(F32)
    for way in (0, 1):
        total += za[rows(za_row(0, way, 2), S), :].astype(F32)
    ig_ref[...] = total
    got(s0[0], *near0, y_x)

    @pl.loop(0, S // 16)
    def _(i):
        at = rows(i * 16, 16)
        total = p[rows(wrow(0, 0) + i * 16, 16), :].astype(F32)
        total += sib[rows((dp_at(0, 0) // 2) * S + i * 16, 16), :].astype(F32)
        for way in (0, 1):
            total += yb[rows(yb_row(0, way) + i * 16, 16), :].astype(F32)
        grad_ref[at, :] = total + xb[at, :].astype(F32)

    for copy in sent:
        copy.wait_send()


def moments(m, v, grad):
    m_new = 0.9 * m + 0.1 * grad
    v_new = 0.95 * v + 0.05 * grad * grad
    return m_new, v_new, m_new / (jnp.sqrt(v_new) + 1e-8)


def finish(dp_ref, grad_ref, ig_ref, mask_ref, mgu_ref, vgu_ref, md_ref, vd_ref,
           out_ref, mgu_new, vgu_new, sgu, md_new, vd_new, sd):
    keep = keep_of(mask_ref, dp_ref[0])
    scale = jnp.float32(8192.0) ** -0.5
    rest = grad_ref[:, 2 * MAIN : GU]
    for k in (0, 1):
        tail = (rest if k == 0 else pltpu.roll(rest, 64, 1))[:, : F - MAIN]
        grad = jnp.concatenate([grad_ref[:, k * MAIN : (k + 1) * MAIN], tail], 1)
        grad = jnp.where(keep != 0, grad * scale, 0.0)
        mgu_new[k], vgu_new[k], sgu[k] = moments(mgu_ref[k], vgu_ref[k], grad)
    grad = jnp.where(keep != 0, grad_ref[:, GU : GU + F] * scale, 0.0).T
    md_new[...], vd_new[...], sd[...] = moments(md_ref[...], vd_ref[...], grad)
    out_ref[...] = ig_ref[...].T.astype(BF)


def on_device(tokens, cotangent, mask, wgu, wd, mgu, vgu, md, vd):
    vmem = pl.BlockSpec(memory_space=pltpu.VMEM)
    sds = jax.ShapeDtypeStruct
    grad, ig = pl.pallas_call(
        body,
        name="ffn_grads",
        out_shape=(sds((S, PK), F32), sds((S, T), F32)),
        in_specs=[vmem] * 5,
        out_specs=(vmem, vmem),
        scratch_shapes=[
            pltpu.VMEM((D, 2 * T), BF),
            pltpu.VMEM((D, PK), BF),
            pltpu.VMEM((D, PK), BF),
            pltpu.VMEM((T, GU), BF),
            pltpu.VMEM((T, 640), BF),
            pltpu.VMEM((D, T), BF),
            pltpu.VMEM((8 * S, PK), BF),
            pltpu.VMEM((4 * 80, PK), BF),
            pltpu.VMEM((4 * S, PK), BF),
            pltpu.VMEM((S, PK), BF),
            pltpu.VMEM((12 * S, T), BF),
            pltpu.VMEM((4 * 80, T), BF),
            pltpu.VMEM((S, T), BF),
            pltpu.SemaphoreType.DMA((COPIES,)),
            pltpu.SemaphoreType.DMA((COPIES,)),
        ],
        compiler_params=pltpu.CompilerParams(
            collective_id=0, has_side_effects=True, vmem_limit_bytes=58 << 20
        ),
    )(tokens, cotangent, mask, wgu, wd)
    dp = lax.axis_index("dp").astype(jnp.int32).reshape(1)
    big, down = sds((2, S, F), F32), sds((F, S), F32)
    return pl.pallas_call(
        finish,
        name="moments",
        out_shape=(sds((T, S), BF), big, big, big, down, down, down),
        in_specs=[pl.BlockSpec(memory_space=pltpu.SMEM)] + [vmem] * 7,
        out_specs=(vmem,) * 7,
        compiler_params=pltpu.CompilerParams(vmem_limit_bytes=40 << 20),
    )(dp, grad, ig, mask, mgu, vgu, md, vd)


def solution(mesh):
    return jax.shard_map(
        on_device,
        mesh=mesh,
        in_specs=(
            P("dp", "tensor"),
            P("dp", "tensor"),
            P(None, "tensor"),
            P(None, "dp", "tensor"),
            P("tensor", "dp"),
            P(None, "dp", "tensor"),
            P(None, "dp", "tensor"),
            P("tensor", "dp"),
            P("tensor", "dp"),
        ),
        out_specs=(
            P("dp", "tensor"),
            P(None, "dp", "tensor"),
            P(None, "dp", "tensor"),
            P(None, "dp", "tensor"),
            P("tensor", "dp"),
            P("tensor", "dp"),
            P("tensor", "dp"),
        ),
        check_vma=False,
    )
```

time: 743 us -> 135 us (0.18)
  waiting for transfers between devices: 638 us -> 0 us
  Pallas kernels: 0 us -> 118 us
  matrix products: 33.8 us -> 0 us
  local copies, waits for them, and re-layouts: 45.2 us -> 15.9 us
  between operations: 14.9 us -> 0.71 us
  other arithmetic: 8.67 us -> 0 us
    unnamed x8 -> x0, waiting for transfers between devices: 270 us -> none
    all_gather x4 -> x0, waiting for transfers between devices: 232 us -> none  [the longest x1 64.9 us: on_device(): lax.all_gather(w_gate_up, 'dp', axis=1, tiled=True)]
    reduce_scatter x2 -> x0, waiting for transfers between devices: 137 us -> none  [the longest x1 81.2 us: on_device(): lax.psum_scatter(partial_input, 'tensor', scatter_dimension=1, tiled=True)]
    pallas_call x0 -> x2, Pallas kernels: none -> 118 us  [the longest x1 116 us: on_device(): pl.pallas_call(body, name='ffn_grads', out_shape=(sds((S, PK), F32), sds(...]
    dot_general x5 -> x0, matrix products: 33.8 us -> none  [the longest x1 9.18 us: on_device(): jnp.einsum('td,ktf->kdf', features, both_grads, preferred_element_type=jn...]
    transpose x1 -> x0, local copies, waits for them, and re-layouts: 19.4 us -> none  [on_device(): jnp.einsum('td,ktf->kdf', features, both_grads, preferred_element_type=jn...]
    all_gather x1 -> x0, local copies, waits for them, and re-layouts: 16.6 us -> none  [on_device(): lax.all_gather(w_gate_up, 'dp', axis=1, tiled=True)]
  transfers between devices with their start and end apart: 7 -> 0, of which waited for: 7 -> 0; matrix products, arithmetic and copies ran while one was open for 11% -> 0% of each run, Pallas kernels for 0% -> 0%
where the time goes in v1:
time: 135 us
  Pallas kernels  118 us (87%)
  local copies, waits for them, and re-layouts  15.9 us (12%)
    pallas_call x1, Pallas kernels, on_device(): pl.pallas_call(body, name='ffn_grads', out_shape=(sds((S, PK), F32), sds(...  116 us
    unnamed x31, local copies, waits for them, and re-layouts  10.2 us
    pallas_call x4, local copies, waits for them, and re-layouts, on_device(): pl.pallas_call(finish, name='moments', out_shape=(sds((T, S), BF), big, b...  5.68 us

profile of v1, /device:TPU:2, one launch (start us, length us, event | category | flops | bytes accessed | tf_op | source)
XLA Modules:
  0.0 134.6 jit_solution(1527049559156194376)
XLA Ops:
  0.6 0.0 copy-start.12
  0.6 1.8 %copy.16.tok_ref = bf16[512,144]{1,0:T(8,128)(2,1)} copy(bf16[512,144]{0,1:T(8,128)(2,1)} %param.9) | data formatting | bytes 294912 | tf_op args[0]
  2.4 0.0 copy-done.12
  2.4 0.0 copy-start.11
  2.4 0.8 copy.17.cot_ref
  3.3 0.1 copy-done.11
  3.4 0.9 copy.18.wd_ref
  4.2 0.0 copy-start.9
  4.2 0.0 copy-start.10
  4.2 116.0 %ffn_grads.1 = (f32[144,1792]{1,0:T(8,128)}, f32[144,512]{1,0:T(8,128)}) custom-call(bf16[512,144]{1,0:T(8,128)(2,1)} %copy.16.tok_ref, bf16[512,144]{1,0:T(8,128)(2,1)} %copy.17.cot_ref, s32[18,576]{1,0:T(8,128)} %mask_ref.3, bf16[2,144,576]{2,1,0:T(8,128)(2,1)} %wgu_ref.1, bf16[576,144]{1,0:T(8,128)(2,1)} %copy.18.wd_ref), custom_call_target="tpu_custom_call" | custom-call | tf_op jit(solution)/shard_map/ffn_grads/pallas_call | solution.py:342
  120.2 0.0 copy-start
  120.2 0.0 copy-done.9
  120.3 0.0 copy-start.1
  120.3 0.2 copy.19.md_ref
  120.5 0.0 copy-done.10
  120.5 0.2 copy.20.vd_ref
  120.7 0.7 copy-done
  121.5 0.2 copy-done.1
  121.7 0.0 copy-start.2
  121.7 1.1 copy-done.2
  122.8 0.0 copy-start.6
  122.8 1.0 copy-done.6
  123.7 0.0 copy-start.8
  123.7 0.8 copy-done.8
  124.6 2.0 %moments.1 = (bf16[512,144]{1,0:T(8,128)(2,1)S(1)}, f32[2,144,576]{2,1,0:T(8,128)}, f32[2,144,576]{2,1,0:T(8,128)}, f32[2,144,576]{2,1,0:T(8,128)}, f32[576,144]...) custom-call(s32[1]{0:T(128)} %bitcast.dp_ref, f32[144,1792]{1,0:T(8,128)S(1)} %copy-done, ...), custom_call_target="tpu_custom_call" | custom-call | tf_op jit(solution)/shard_map/moments/pallas_call | solution.py:371
  126.6 0.0 copy-start.3
  126.6 0.8 copy-done.3
  127.4 0.0 copy-start.5
  127.4 0.8 copy-done.5
  128.3 0.0 copy-start.7
  128.3 0.7 copy-done.7
  129.0 0.0 copy-start.4
  129.0 1.8 %copy.21 = bf16[512,144]{0,1:T(8,128)(2,1)} copy(bf16[512,144]{1,0:T(8,128)(2,1)} %copy-done.7) | data formatting | bytes 294912 | tf_op jit(solution)/shard_map/moments/pallas_call | solution.py:371
  130.8 2.0 %copy.22 = f32[576,144]{0,1:T(8,128)} copy(f32[576,144]{1,0:T(8,128)} %copy-done.5) | data formatting | bytes 663552 | tf_op jit(solution)/shard_map/moments/pallas_call | solution.py:371
  132.8 0.0 copy-done.4
  132.8 0.9 copy.23
  133.7 0.9 copy.24
Async XLA Ops:
  0.6 1.8 %copy-start.12 = (bf16[512,144]{0,1:T(8,128)(2,1)S(1)}, bf16[512,144]{0,1:T(8,128)(2,1)}, u32[]{:S(2)}) copy-start(bf16[512,144]{0,1:T(8,128)(2,1)} %param.10) | copy-start | bytes 442372
  2.4 0.9 copy-start.11
  4.2 116.0 %copy-start.9 = (f32[576,144]{0,1:T(8,128)S(1)}, f32[576,144]{0,1:T(8,128)}, u32[]{:S(2)}) copy-start(f32[576,144]{0,1:T(8,128)} %param.16) | copy-start | bytes 995332
  4.2 116.3 %copy-start.10 = (f32[576,144]{0,1:T(8,128)S(1)}, f32[576,144]{0,1:T(8,128)}, u32[]{:S(2)}) copy-start(f32[576,144]{0,1:T(8,128)} %param.17) | copy-start | bytes 995332
  120.2 1.2 copy-start
  120.3 1.4 %copy-start.1 = (f32[2,144,576]{2,1,0:T(8,128)S(1)}, f32[2,144,576]{2,1,0:T(8,128)}, u32[]{:S(2)}) copy-start(f32[2,144,576]{2,1,0:T(8,128)} %mgu_ref.1) | copy-start | bytes 1990660
  121.7 1.1 copy-start.2
  122.8 1.0 copy-start.6
  123.7 0.8 copy-start.8
  126.6 0.8 copy-start.3
  127.4 0.8 copy-start.5
  128.3 0.7 copy-start.7
  129.0 3.8 %copy-start.4 = (f32[576,144]{1,0:T(8,128)S(1)}, f32[576,144]{1,0:T(8,128)}, u32[]{:S(2)}) copy-start(f32[576,144]{1,0:T(8,128)} %copy-done.3) | copy-start | bytes 995332

commit v2 on v1

--- a/solution.py
+++ b/solution.py
@@ -18,7 +18,9 @@
 GU = 1152
 PK = 1792
 CUTS = (((0, 80), (80, 64)), ((80, 64), (0, 80)))
-COPIES = 80
+PARTS = ((0, 80), (80, 64))
+WAYS = (0, 1)
+COPIES = 96
 
 
 def dot(a, b, ca, cb):
@@ -89,8 +91,8 @@
         h[tok, MAIN:640] = jnp.where(low, hidden, 0.0).astype(BF)
 
 
-def body(tok_ref, cot_ref, mask_ref, wgu_ref, wd_ref, grad_ref, ig_ref,
-         a, w, p, g, h, ig, sib, ya, yb, xb, za, zh, xl, send_sem, recv_sem):
+def body(tok_hbm, cot_hbm, mask_hbm, wgu_hbm, wd_hbm, grad_ref, ig_ref,
+         mask_ref, wgu_ref, wd_ref, in_sem, a, w, p, g, h, ig, sib, ya, yb, xb, za, zh, xl, send_sem, recv_sem):
     dp, tensor = lax.axis_index("dp"), lax.axis_index("tensor")
     y, hi, c = dp // 4, (dp // 2) % 2, dp % 2
     lo, z = tensor // 8, tensor % 8
@@ -107,6 +109,20 @@
     up_z, down_z = (dp, t_at(1, 0)), (dp, t_at(7, 0))
     other_h, other_l, sibling = (dp_at(0, 1), tensor), (dp, t_at(0, 1)), (dp_at(0, 0, 1), tensor)
     ydev, zdev = (up_y, down_y), (up_z, down_z)
+
+    own_a = rows((lo * 8 + z) * S, S)
+    loads = [
+        pltpu.make_async_copy(src, dst, in_sem.at[n])
+        for n, (src, dst) in enumerate((
+            (tok_hbm, a.at[own_a, pl.ds(0, T)]),
+            (cot_hbm, a.at[own_a, pl.ds(T, T)]),
+            (mask_hbm, mask_ref),
+            (wgu_hbm, wgu_ref),
+            (wd_hbm, wd_ref),
+        ))
+    ]
+    for load in loads:
+        load.start()
 
     barrier = pltpu.get_barrier_semaphore()
     partners = (up_y, down_y, up_z, down_z, other_h, other_l, sibling)
@@ -124,6 +140,10 @@
         sent.append(copy)
         return copy
 
+    def drain():
+        for copy in sent:
+            copy.wait_send()
+
     def got(*copies):
         for copy in copies:
             copy.wait_recv()
@@ -138,57 +158,88 @@
     def arow(dz, k):
         return t_at(dz, k) * S
 
-    own_a = rows(arow(0, 0), S)
-    a[own_a, 0:T] = tok_ref[...].T
-    a[own_a, T : 2 * T] = cot_ref[...].T
-    keep = keep_of(mask_ref, dp)
-    pack(w, rows(wrow(0, 0), S), keep, wgu_ref[0], wgu_ref[1], wd_ref[...].T)
+    def part_of(ref, start, part, dev):
+        return same(ref, start + PARTS[part][0], PARTS[part][1], dev)
+
+    def to_sibling(dy, k):
+        w_c.append(same(w, wrow(dy, k), S, sibling))
+
+    for load in loads[:2]:
+        load.wait()
     pl.semaphore_wait(barrier, len(partners))
-
+    w_c = []
     a_x = same(a, arow(0, 0), S, other_l)
-    a0 = [same(a, arow(0, 0), S, d) for d in zdev]
-    w0 = [same(w, wrow(0, 0), S, d) for d in ydev]
-    w_x = same(w, wrow(0, 0), S, other_h)
-    w_c = [same(w, wrow(0, 0), S, sibling)]
-
-    def w_next(k, first):
-        halves = []
-        for way, (copy, dy) in enumerate(zip(first, (3, 1))):
-            got(copy)
-            start, count = CUTS[k][way]
-            halves.append(same(w, wrow(dy, k) + start, count, ydev[way]))
-            w_c.append(same(w, wrow(dy, k), S, sibling))
-        return halves
-
-    def w_last(k, halves):
-        got(*halves)
-        w_c.append(same(w, wrow(2, k), S, sibling))
-
-    def a_next(k, copies, d):
-        out = []
-        for way, (copy, dz) in enumerate(zip(copies, (8 - d, d))):
-            got(copy)
-            start, count = CUTS[k][way] if d == 3 else (0, S)
-            out.append(same(a, arow(dz, k) + start, count, zdev[way]))
-        return out
-
-    a1 = a_next(0, a0, 1)
+    a0, a1, a2, a3, b0, b1 = {}, {}, {}, {}, {}, {}
+    w0, w1, v0, v1 = {}, {}, {}, {}
+    for turn in (0, 1):
+        for way in WAYS:
+            a0[way, turn ^ way] = part_of(a, arow(0, 0), turn ^ way, zdev[way])
+    for load in loads[2:]:
+        load.wait()
+    pack(w, rows(wrow(0, 0), S), keep_of(mask_ref, dp), wgu_ref[0], wgu_ref[1], wd_ref[...])
+    for turn in (0, 1):
+        for way in WAYS:
+            w0[way, turn ^ way] = part_of(w, wrow(0, 0), turn ^ way, ydev[way])
+    w_x = [part_of(w, wrow(0, 0), part, other_h) for part in (0, 1)]
+    to_sibling(0, 0)
+
+    def a_next(copies, out, k, d, part, way):
+        got(copies[way, part])
+        out[way, part] = part_of(a, arow((8 - d, d)[way], k), part, zdev[way])
+
+    def w_next(copies, out, k):
+        for way in WAYS:
+            part = way ^ k
+            got(copies[way, part])
+            out[way, part] = part_of(w, wrow((3, 1)[way], k), part, ydev[way])
+
+    def w_rest(copies, k):
+        for way in WAYS:
+            got(copies[way, 1 - way ^ k])
+            to_sibling((3, 1)[way], k)
+
+    def w_last(copies, k):
+        got(*copies.values())
+        to_sibling(2, k)
+
+    for way in WAYS:
+        a_next(a0, a1, 0, 1, way, way)
+    w_next(w0, w1, 0)
+    for way in WAYS:
+        a_next(a0, a1, 0, 1, 1 - way, way)
+    for way in WAYS:
+        a_next(a1, a2, 0, 2, way, way)
+    w_rest(w0, 0)
+    for way in WAYS:
+        a_next(a1, a2, 0, 2, 1 - way, way)
     got(a_x)
-    b0 = [same(a, arow(0, 1), S, d) for d in zdev]
-    w1 = w_next(0, w0)
-    got(w_x)
-    v0 = [same(w, wrow(0, 1), S, d) for d in ydev]
-    w_c.append(same(w, wrow(0, 1), S, sibling))
-    a2 = a_next(0, a1, 2)
-    b1 = a_next(1, b0, 1)
-    w_last(0, w1)
-    a3 = a_next(0, a2, 3)
-    a_l = [same(a, arow(dz, 0), S, other_l) for dz in (5, 3)]
-    v1 = w_next(1, v0)
-    got(*a3)
-    a_l.append(same(a, arow(4, 0), S, other_l))
-    got(*b1)
-    w_last(1, v1)
+    for part in (0, 1):
+        for way in WAYS:
+            b0[way, part] = part_of(a, arow(0, 1), part, zdev[way])
+    for part in (0, 1):
+        got(w_x[part])
+        for way in WAYS:
+            v0[way, part] = part_of(w, wrow(0, 1), part, ydev[way])
+    to_sibling(0, 1)
+    a_l = []
+    for way in WAYS:
+        a_next(a2, a3, 0, 3, way, way)
+        a_l.append(part_of(a, arow((5, 3)[way], 0), way, other_l))
+    w_last(w1, 0)
+    for way in WAYS:
+        got(a2[way, 1 - way])
+        a_l.append(part_of(a, arow((5, 3)[way], 0), 1 - way, other_l))
+    for way in WAYS:
+        a_next(b0, b1, 1, 1, 0, way)
+    for way in WAYS:
+        got(a3[way, way])
+        a_l.append(part_of(a, arow(4, 0), way, other_l))
+    w_next(v0, v1, 1)
+    for way in WAYS:
+        a_next(b0, b1, 1, 1, 1, way)
+    w_rest(v0, 1)
+    got(*b1.values())
+    w_last(v1, 1)
     got(*a_l, *w_c)
 
     hidden_pass(a, w, g, h)
@@ -235,22 +286,8 @@
             out.append(y_near(k, way, way))
         return out
 
-    s2 = weight_grads(2)
-    s1 = weight_grads(1)
-    with_sibling(2, 1, s2)
-    far1 = y_far(1)
-    s3 = weight_grads(3)
-    with_sibling(1, 1, s1)
-    near1 = [y_near(1, 0, 1)]
-    with_sibling(3, 1, s3)
-    near1.append(y_near(1, 1, 0))
-    with_sibling(2, 0, s2)
-    far0 = y_far(0)
-    s0 = weight_grads(0)
-
-    @pl.loop(0, 2)
-    def _(i):
-        at = rows(i * 1152, 1152)
+    def input_grad(k):
+        at = rows(lk[k] * 1152, 1152)
         ig[at, :] = dot(w[at, 0:GU], g[...], 1, 1).astype(BF)
 
     def za_row(k, way, step):
@@ -277,23 +314,41 @@
             out.append(send(src, za.at[rows(za_row(k, way, 3 - d), S)], zdev[way]))
         return out
 
-    zc = {k: z_far(k) for k in (1, 0)}
+    s2 = weight_grads(2)
+    s1 = weight_grads(1)
+    with_sibling(2, 1, s2)
+    far1 = y_far(1)
+    s3 = weight_grads(3)
+    with_sibling(1, 1, s1)
+    near1 = [y_near(1, 0, 1)]
+    input_grad(1)
+    zc = {1: z_far(1)}
+    with_sibling(3, 1, s3)
+    near1.append(y_near(1, 1, 0))
+    with_sibling(2, 0, s2)
+    input_grad(0)
+    zc[0] = z_far(0)
     near1 += y_pass(1, far1)
-    zc = {k: z_pass(k, zc[k], 3) for k in (1, 0)}
+    far0 = y_far(0)
     with_sibling(1, 0, s1)
     near0 = [y_near(0, 0, 1)]
     with_sibling(3, 0, s3)
     near0.append(y_near(0, 1, 0))
-    zc = {k: z_pass(k, zc[k], 2) for k in (1, 0)}
-    near0 += y_pass(0, far0)
-    zc = {k: z_pass(k, zc[k], 1) for k in (1, 0)}
-    got(*zc[1])
-    add_rows(ig, arow(0, 1), S, (za, za_row(1, 0, 2)), (za, za_row(1, 1, 2)))
-    z_x = send(ig.at[rows(arow(0, 1), S)], xl, other_l)
+    zc[1] = z_pass(1, zc[1], 3)
+    s0 = weight_grads(0)
+    zc[0] = z_pass(0, zc[0], 3)
+    zc[1] = z_pass(1, zc[1], 2)
+    zc[0] = z_pass(0, zc[0], 2)
     got(s0[1], *near1)
     own = (dp_at(0, 1) // 2) * S
     add_rows(p, wrow(0, 1), S, (sib, own), (yb, yb_row(1, 0)), (yb, yb_row(1, 1)))
     y_x = send(p.at[rows(wrow(0, 1), S)], xb, other_h)
+    near0 += y_pass(0, far0)
+    zc[1] = z_pass(1, zc[1], 1)
+    zc[0] = z_pass(0, zc[0], 1)
+    got(*zc[1])
+    add_rows(ig, arow(0, 1), S, (za, za_row(1, 0, 2)), (za, za_row(1, 1, 2)))
+    z_x = send(ig.at[rows(arow(0, 1), S)], xl, other_l)
 
     got(*zc[0], z_x)
     total = ig[rows(arow(0, 0), S), :].astype(F32) + xl[...].astype(F32)
@@ -311,8 +366,7 @@
             total += yb[rows(yb_row(0, way) + i * 16, 16), :].astype(F32)
         grad_ref[at, :] = total + xb[at, :].astype(F32)
 
-    for copy in sent:
-        copy.wait_send()
+    drain()
 
 
 def moments(m, v, grad):
@@ -321,31 +375,69 @@
     return m_new, v_new, m_new / (jnp.sqrt(v_new) + 1e-8)
 
 
-def finish(dp_ref, grad_ref, ig_ref, mask_ref, mgu_ref, vgu_ref, md_ref, vd_ref,
-           out_ref, mgu_new, vgu_new, sgu, md_new, vd_new, sd):
-    keep = keep_of(mask_ref, dp_ref[0])
+def finish(dp_ref, grad_hbm, ig_hbm, mask_hbm, mgu_hbm, vgu_hbm, md_hbm, vd_hbm,
+           out_hbm, mgu_new, vgu_new, sgu_new, md_new, vd_new, sd_new,
+           grad_ref, ig_ref, mask, out, old, new, in_sem, out_sem):
+    firsts = (mgu_hbm.at[0], mgu_hbm.at[1], md_hbm)
+    seconds = (vgu_hbm.at[0], vgu_hbm.at[1], vd_hbm)
+    loads = [
+        pltpu.make_async_copy(mask_hbm, mask, in_sem.at[6]),
+        pltpu.make_async_copy(grad_hbm, grad_ref, in_sem.at[7]),
+        pltpu.make_async_copy(ig_hbm, ig_ref, in_sem.at[8]),
+    ]
+    for k in range(3):
+        loads.append(pltpu.make_async_copy(firsts[k], old.at[2 * k], in_sem.at[2 * k]))
+        loads.append(pltpu.make_async_copy(seconds[k], old.at[2 * k + 1], in_sem.at[2 * k + 1]))
+    for load in loads:
+        load.start()
+    loads[2].wait()
+    out[...] = ig_ref[...].astype(BF)
+    stores = [pltpu.make_async_copy(out, out_hbm, out_sem.at[9])]
+    stores[0].start()
+    loads[0].wait()
+    loads[1].wait()
     scale = jnp.float32(8192.0) ** -0.5
+    keep = jnp.where(keep_of(mask, dp_ref[0]) != 0, scale, 0.0)
     rest = grad_ref[:, 2 * MAIN : GU]
-    for k in (0, 1):
-        tail = (rest if k == 0 else pltpu.roll(rest, 64, 1))[:, : F - MAIN]
-        grad = jnp.concatenate([grad_ref[:, k * MAIN : (k + 1) * MAIN], tail], 1)
-        grad = jnp.where(keep != 0, grad * scale, 0.0)
-        mgu_new[k], vgu_new[k], sgu[k] = moments(mgu_ref[k], vgu_ref[k], grad)
-    grad = jnp.where(keep != 0, grad_ref[:, GU : GU + F] * scale, 0.0).T
-    md_new[...], vd_new[...], sd[...] = moments(md_ref[...], vd_ref[...], grad)
-    out_ref[...] = ig_ref[...].T.astype(BF)
-
-
-def on_device(tokens, cotangent, mask, wgu, wd, mgu, vgu, md, vd):
-    vmem = pl.BlockSpec(memory_space=pltpu.VMEM)
-    sds = jax.ShapeDtypeStruct
-    grad, ig = pl.pallas_call(
+    results = ((mgu_new.at[0], vgu_new.at[0], sgu_new.at[0]),
+               (mgu_new.at[1], vgu_new.at[1], sgu_new.at[1]),
+               (md_new, vd_new, sd_new))
+    for k in range(3):
+        if k < 2:
+            tail = (rest if k == 0 else pltpu.roll(rest, 64, 1))[:, : F - MAIN]
+            grad = jnp.concatenate([grad_ref[:, k * MAIN : (k + 1) * MAIN], tail], 1)
+        else:
+            grad = grad_ref[:, GU : GU + F]
+        loads[3 + 2 * k].wait()
+        loads[4 + 2 * k].wait()
+        new[3 * k], new[3 * k + 1], new[3 * k + 2] = moments(
+            old[2 * k], old[2 * k + 1], grad * keep
+        )
+        for n in range(3):
+            store = pltpu.make_async_copy(new.at[3 * k + n], results[k][n], out_sem.at[3 * k + n])
+            store.start()
+            stores.append(store)
+    for store in stores:
+        store.wait()
+
+
+VMEM = pl.BlockSpec(memory_space=pltpu.VMEM)
+HBM = pl.BlockSpec(memory_space=pltpu.HBM)
+sds = jax.ShapeDtypeStruct
+
+
+def ffn(tokens, cotangent, mask, wgu, wd):
+    return pl.pallas_call(
         body,
         name="ffn_grads",
         out_shape=(sds((S, PK), F32), sds((S, T), F32)),
-        in_specs=[vmem] * 5,
-        out_specs=(vmem, vmem),
+        in_specs=[HBM] * 5,
+        out_specs=(VMEM, VMEM),
         scratch_shapes=[
+            pltpu.VMEM(mask.shape, jnp.int32),
+            pltpu.VMEM(wgu.shape, BF),
+            pltpu.VMEM(wd.shape, BF),
+            pltpu.SemaphoreType.DMA((5,)),
             pltpu.VMEM((D, 2 * T), BF),
             pltpu.VMEM((D, PK), BF),
             pltpu.VMEM((D, PK), BF),
@@ -363,19 +455,34 @@
             pltpu.SemaphoreType.DMA((COPIES,)),
         ],
         compiler_params=pltpu.CompilerParams(
-            collective_id=0, has_side_effects=True, vmem_limit_bytes=58 << 20
+            collective_id=0, has_side_effects=True, vmem_limit_bytes=62 << 20
         ),
     )(tokens, cotangent, mask, wgu, wd)
+
+
+def on_device(tokens, cotangent, mask, wgu, wd, mgu, vgu, md, vd):
+    grad, ig = ffn(tokens.T, cotangent.T, mask, wgu, wd.T)
     dp = lax.axis_index("dp").astype(jnp.int32).reshape(1)
-    big, down = sds((2, S, F), F32), sds((F, S), F32)
-    return pl.pallas_call(
+    big, down = sds((2, S, F), F32), sds((S, F), F32)
+    out = pl.pallas_call(
         finish,
         name="moments",
-        out_shape=(sds((T, S), BF), big, big, big, down, down, down),
-        in_specs=[pl.BlockSpec(memory_space=pltpu.SMEM)] + [vmem] * 7,
-        out_specs=(vmem,) * 7,
-        compiler_params=pltpu.CompilerParams(vmem_limit_bytes=40 << 20),
-    )(dp, grad, ig, mask, mgu, vgu, md, vd)
+        out_shape=(sds((S, T), BF), big, big, big, down, down, down),
+        in_specs=[pl.BlockSpec(memory_space=pltpu.SMEM)] + [HBM] * 7,
+        out_specs=(HBM,) * 7,
+        scratch_shapes=[
+            pltpu.VMEM((S, PK), F32),
+            pltpu.VMEM((S, T), F32),
+            pltpu.VMEM(mask.shape, jnp.int32),
+            pltpu.VMEM((S, T), BF),
+            pltpu.VMEM((6, S, F), F32),
+            pltpu.VMEM((9, S, F), F32),
+            pltpu.SemaphoreType.DMA((9,)),
+            pltpu.SemaphoreType.DMA((10,)),
+        ],
+        compiler_params=pltpu.CompilerParams(vmem_limit_bytes=62 << 20),
+    )(dp, grad, ig, mask, mgu, vgu, md.T, vd.T)
+    return (out[0].T, *out[1:4], *(x.T for x in out[4:]))
 
 
 def solution(mesh):

time: 135 us -> 102 us (0.76)
  Pallas kernels: 118 us -> 101 us
  local copies, waits for them, and re-layouts: 15.9 us -> 0 us
    pallas_call x2, Pallas kernels: 118 us -> 101 us  [the longest x1 97.6 us: ffn(): pl.pallas_call(body, name='ffn_grads', out_shape=(sds((S, PK), F32), sds(...]
    unnamed x31 -> x0, local copies, waits for them, and re-layouts: 10.2 us -> none
    pallas_call x4 -> x0, local copies, waits for them, and re-layouts: 5.68 us -> none  [on_device(): pl.pallas_call(finish, name='moments', out_shape=(sds((T, S), BF), big, b...]
where the time goes in v2:
time: 102 us
  Pallas kernels  101 us (99%)
    pallas_call x1, Pallas kernels, ffn(): pl.pallas_call(body, name='ffn_grads', out_shape=(sds((S, PK), F32), sds(...  97.6 us
    pallas_call x1, Pallas kernels, on_device(): pl.pallas_call(finish, name='moments', out_shape=(sds((S, T), BF), big, b...  3.76 us

profile of v2, /device:TPU:2, one launch (start us, length us, event | category | flops | bytes accessed | tf_op | source)
XLA Modules:
  0.0 102.0 jit_solution(9715854076070463066)
XLA Ops:
  0.6 97.6 %ffn_grads.1 = (f32[144,1792]{1,0:T(8,128)}, f32[144,512]{1,0:T(8,128)}) custom-call(bf16[144,512]{1,0:T(8,128)(2,1)} %bitcast.13, bf16[144,512]{1,0:T(8,128)(2,1)} %bitcast.14, s32[18,576]{1,0:T(8,128)} %mask_hbm.3, bf16[2,144,576]{2,1,0:T(8,128)(2,1)} %wgu_hbm.1, bf16[144,576]{1,0:T(8,128)(2,1)} %bitcast.12), custom_call_target="tpu_custom_call" | custom-call | tf_op jit(solution)/shard_map/ffn_grads/pallas_call | solution.py:430
  98.2 3.8 %moments.1 = (bf16[144,512]{1,0:T(8,128)(2,1)}, f32[2,144,576]{2,1,0:T(8,128)}, f32[2,144,576]{2,1,0:T(8,128)}, f32[2,144,576]{2,1,0:T(8,128)}, f32[144,576]{1,0...) custom-call(s32[1]{0:T(128)} %bitcast.dp_ref, f32[144,1792]{1,0:T(8,128)} %get-tuple-element.16.grad_hbm, ...), custom_call_target="tpu_custom_call" | custom-call | tf_op jit(solution)/shard_map/moments/pallas_call | solution.py:467

commit v3 on v2

v3 whole, which is shorter than its diff:
```python
import functools
import jax
import jax.numpy as jnp
from jax import lax
from jax.experimental import pallas as pl
from jax.experimental.pallas import tpu as pltpu
from jax.sharding import PartitionSpec as P

BF = jnp.bfloat16
F32 = jnp.float32
MESH = pl.DeviceIdType.MESH

D = 2304
S = 144
T = 512
F = 576
MAIN = 512
PK = 1792
HALF = ((0, 768), (768, 1024))
GLANES = ((0, 512), (512, 640))
HLANES = ((0, 256), (256, 384))
CUTS = (((0, 80), (80, 64)), ((80, 64), (0, 80)))
PARTS = ((0, 80), (80, 64))
WAYS = (0, 1)
COPIES = 128


def dot(a, b, ca, cb):
    return lax.dot_general(a, b, (((ca,), (cb,)), ((), ())), preferred_element_type=F32)


def rows(start, count, step=16):
    return pl.ds(pl.multiple_of(start, step), count)


def keep_of(mask_ref, dp):
    block = dp + dp // 8
    first = 128 - 16 * (dp % 8)
    row = lax.broadcasted_iota(jnp.int32, (S, F), 0)
    return jnp.where(row < first, mask_ref[pl.ds(block, 1), :], mask_ref[pl.ds(block + 1, 1), :])


def pack(ref, at, keep, gate, up, down):
    gate, up, down = (jnp.where(keep != 0, w.astype(F32), 0.0) for w in (gate, up, down))
    at_lane = 0
    rest = jnp.concatenate([gate[:, MAIN:], up[:, MAIN:]], 1)
    last = jnp.concatenate([down[:, MAIN:], jnp.zeros_like(down[:, MAIN:])], 1)
    for part in (gate[:, :256], up[:, :256], down[:, :256], gate[:, 256:MAIN], up[:, 256:MAIN],
                 rest, down[:, 256:MAIN], last):
        ref[at, at_lane : at_lane + part.shape[1]] = part.astype(BF)
        at_lane += part.shape[1]


def add_rows(dst, to, n, lanes, *srcs):
    cols = pl.ds(*lanes)

    @pl.loop(0, n // 16)
    def _(i):
        at = rows(to + i * 16, 16)
        total = dst[at, cols].astype(F32)
        for src, start in srcs:
            total += src[rows(start + i * 16, 16), cols].astype(F32)
        dst[at, cols] = total.astype(dst.dtype)


def grads_of(gate, up, hidden_grad):
    sig = jax.nn.sigmoid(gate)
    silu = gate * sig
    gate_grad = hidden_grad * up * (sig * (1.0 + gate * (1.0 - sig)))
    return gate_grad, hidden_grad * silu, silu * up


def hidden_pass(a, w, g, h, half, m):
    tok = rows(m * 256, 256, 256)
    cot = rows(T + m * 256, 256, 256)
    first, (gl, gn), (hl, hn) = HALF[half][0], GLANES[half], HLANES[half]
    both = dot(a[:, tok], w[:, first : first + gn], 0, 0)
    hg = dot(a[:, cot], w[:, first + gn : first + gn + hn], 0, 0)
    gate_grad, up_grad, hidden = grads_of(both[:, :256], both[:, 256:512], hg[:, :256])
    g[tok, gl : gl + 256] = gate_grad.astype(BF)
    g[tok, gl + 256 : gl + 512] = up_grad.astype(BF)
    h[tok, hl : hl + 256] = hidden.astype(BF)
    if half == 1:
        both, hg = both[:, 512:], hg[:, 256:]
        gate_grad, up_grad, hidden = grads_of(both, pltpu.roll(both, 64, 1), hg)
        low = lax.broadcasted_iota(jnp.int32, (256, 128), 1) < 64
        g[tok, 1024:1152] = jnp.where(low, gate_grad, pltpu.roll(up_grad, 64, 1)).astype(BF)
        h[tok, 512:640] = jnp.where(low, hidden, 0.0).astype(BF)


def body(tok_hbm, cot_hbm, mask_hbm, wgu_hbm, wd_hbm, grad_ref, ig_ref,
         mask_ref, wgu_ref, wd_ref, in_sem, a, w, p, g, h, ig, sib, ya, yb, xb, xq, za, zh, xl, send_sem, recv_sem):
    dp, tensor = lax.axis_index("dp"), lax.axis_index("tensor")
    y, hi, c = dp // 4, (dp // 2) % 2, dp % 2
    lo, z = tensor // 8, tensor % 8
    hk = (hi, 1 - hi)
    lk = (lo, 1 - lo)

    def dp_at(dy, k, flip=0):
        return (((y + dy) % 4) * 2 + hk[k]) * 2 + (1 - c if flip else c)

    def t_at(dz, k):
        return lk[k] * 8 + (z + dz) % 8

    up_y, down_y = (dp_at(1, 0), tensor), (dp_at(3, 0), tensor)
    up_z, down_z = (dp, t_at(1, 0)), (dp, t_at(7, 0))
    other_h, other_l, sibling = (dp_at(0, 1), tensor), (dp, t_at(0, 1)), (dp_at(0, 0, 1), tensor)
    ydev, zdev = (up_y, down_y), (up_z, down_z)

    own_a = rows((lo * 8 + z) * S, S)
    loads = [
        pltpu.make_async_copy(src, dst, in_sem.at[n])
        for n, (src, dst) in enumerate((
            (tok_hbm, a.at[own_a, pl.ds(0, T)]),
            (cot_hbm, a.at[own_a, pl.ds(T, T)]),
            (mask_hbm, mask_ref),
            (wgu_hbm, wgu_ref),
            (wd_hbm, wd_ref),
        ))
    ]
    for load in loads:
        load.start()

    barrier = pltpu.get_barrier_semaphore()
    partners = (up_y, down_y, up_z, down_z, other_h, other_l, sibling)
    for dev in partners:
        pl.semaphore_signal(barrier, inc=1, device_id=dev, device_id_type=MESH)

    sent = []

    def send(src, dst, dev):
        n = len(sent)
        copy = pltpu.make_async_remote_copy(
            src, dst, send_sem.at[n], recv_sem.at[n], device_id=dev, device_id_type=MESH
        )
        copy.start()
        sent.append(copy)
        return copy

    def drain():
        for copy in sent:
            copy.wait_send()

    def got(*copies):
        for copy in copies:
            copy.wait_recv()

    def same(ref, start, count, dev):
        part = ref.at[rows(start, count)]
        return send(part, part, dev)

    def wrow(dy, k, flip=0):
        return dp_at(dy, k, flip) * S

    def arow(dz, k):
        return t_at(dz, k) * S

    def part(ref, start, count, half):
        return ref.at[rows(start, count), pl.ds(*HALF[half])]

    def part_of(ref, start, part, dev):
        return same(ref, start + PARTS[part][0], PARTS[part][1], dev)

    def to_sibling(dy, k):
        w_c.append(same(w, wrow(dy, k), S, sibling))

    for load in loads:
        load.wait()
    pack(w, rows(wrow(0, 0), S), keep_of(mask_ref, dp), wgu_ref[0], wgu_ref[1], wd_ref[...])
    pl.semaphore_wait(barrier, len(partners))
    core_w = ([], [])
    a_x = same(a, arow(0, 0), S, other_l)
    a0, a1, a2, a3, b0, b1 = {}, {}, {}, {}, {}, {}
    w0, w1, v0, v1, w_x = {}, {}, {}, {}, {}

    def w_send(start, count, half, dev):
        src = part(w, start, count, half)
        return send(src, src, dev)

    def to_sibling(dy, k, half):
        core_w[half].append(w_send(wrow(dy, k), S, half, sibling))

    def w_start(out, k, half):
        for way in WAYS:
            out[way, half] = w_send(wrow(0, k), S, half, ydev[way])

    def w_next(copies, out, k, half):
        for way in WAYS:
            got(copies[way, half])
            start, count = CUTS[k][way]
            out[way, half] = w_send(wrow((3, 1)[way], k) + start, count, half, ydev[way])
            to_sibling((3, 1)[way], k, half)

    def w_last(copies, k, half):
        got(copies[0, half], copies[1, half])
        to_sibling(2, k, half)

    def a_next(copies, out, k, d, part, way):
        got(copies[way, part])
        out[way, part] = part_of(a, arow((8 - d, d)[way], k), part, zdev[way])

    for turn in (0, 1):
        for way in WAYS:
            a0[way, turn ^ way] = part_of(a, arow(0, 0), turn ^ way, zdev[way])
    for half in (0, 1):
        w_start(w0, 0, half)
        w_x[half] = w_send(wrow(0, 0), S, half, other_h)
    for half in (0, 1):
        to_sibling(0, 0, half)
    for way in WAYS:
        a_next(a0, a1, 0, 1, way, way)
    w_next(w0, w1, 0, 0)
    for way in WAYS:
        a_next(a0, a1, 0, 1, 1 - way, way)
    for way in WAYS:
        a_next(a1, a2, 0, 2, way, way)
    w_next(w0, w1, 0, 1)
    got(w_x[0])
    w_start(v0, 1, 0)
    to_sibling(0, 1, 0)
    for way in WAYS:
        a_next(a1, a2, 0, 2, 1 - way, way)
    got(a_x)
    for turn in (0, 1):
        for way in WAYS:
            b0[way, turn] = part_of(a, arow(0, 1), turn, zdev[way])
    a_l = []
    for way in WAYS:
        a_next(a2, a3, 0, 3, way, way)
        a_l.append(part_of(a, arow((5, 3)[way], 0), way, other_l))
    got(w_x[1])
    w_start(v0, 1, 1)
    to_sibling(0, 1, 1)
    w_last(w1, 0, 0)
    for way in WAYS:
        got(a2[way, 1 - way])
        a_l.append(part_of(a, arow((5, 3)[way], 0), 1 - way, other_l))
    w_last(w1, 0, 1)
    for way in WAYS:
        a_next(b0, b1, 1, 1, 0, way)
    for way in WAYS:
        got(a3[way, way])
        a_l.append(part_of(a, arow(4, 0), way, other_l))
    w_next(v0, v1, 1, 0)
    for way in WAYS:
        a_next(b0, b1, 1, 1, 1, way)
    w_next(v0, v1, 1, 1)
    w_last(v1, 1, 0)
    got(*b1.values())
    w_last(v1, 1, 1)
    got(*a_l, *core_w[0])

    def sib_row(dy, k):
        return (dp_at(dy, k) // 2) * S

    def yb_row(k, way):
        return (k * 2 + way) * S

    def weight_product(at, half):
        first, (gl, gn), (hl, hn) = HALF[half][0], GLANES[half], HLANES[half]
        p[at, first : first + gn] = dot(a[at, 0:T], g[:, gl : gl + gn], 1, 0).astype(BF)
        p[at, first + gn : first + gn + hn] = dot(
            a[at, T : 2 * T], h[:, hl : hl + hn], 1, 0
        ).astype(BF)

    def core_copy(dy, k, half, n):
        return pltpu.make_async_remote_copy(
            part(p, wrow(dy, k, 1), S, half), part(sib, sib_row(dy, k), S, half),
            send_sem.at[n], recv_sem.at[n], device_id=sibling, device_id_type=MESH,
        )

    def weight_grads(dys, k, half):
        n0 = len(sent)
        step = (dys[1] - dys[0]) % 4 if len(dys) > 1 else 0
        third = dys[2] - dys[0] - 2 * step if len(dys) > 2 else 0
        for q, dy in enumerate(dys):
            copy = core_copy(dy, k, half, n0 + q)
            sent.append(copy)
            core[dy, k, half] = copy

        @pl.loop(0, len(dys))
        def _(q):
            dy = dys[0] + step * q + third * (q // 2) + 8
            weight_product(rows(sib_row(dy, k) * 2, 2 * S), half)
            core_copy(dy, k, half, n0 + q).start()

    def with_sibling(dy, k, half, *srcs):
        got(core[dy, k, half])
        add_rows(p, wrow(dy, k), S, HALF[half], (sib, sib_row(dy, k)), *srcs)

    def x_far(half):
        with_sibling(2, 1, half)
        far_x[half] = send(part(p, wrow(2, 1), S, half), part(xq, 0, S, half), other_h)

    def y_part(k, way, half, start, count):
        src = part(p, wrow((1, 3)[way], k) + start, count, half)
        return send(src, part(yb, yb_row(k, way) + start, count, half), ydev[way])

    def y_other(half):
        for way in WAYS:
            with_sibling((1, 3)[way], 1, half)
            near1[way, half] = y_part(1, way, half, 0, S)

    def y_near(half):
        for way in WAYS:
            with_sibling((1, 3)[way], 0, half)
            near0[way, half] = y_part(0, way, half, *CUTS[0][1 - way])

    def y_far(half):
        got(far_x[half])
        with_sibling(2, 0, half, (xq, 0))
        for way in WAYS:
            start, count = CUTS[0][way]
            src = part(p, wrow(2, 0) + start, count, half)
            far0[way, half] = send(src, part(ya, way * 80, count, half), ydev[way])

    def y_pass(half):
        for way in WAYS:
            got(far0[way, half])
            start, count = CUTS[0][way]
            to = wrow((1, 3)[way], 0) + start
            add_rows(p, to, count, HALF[half], (ya, way * 80))
            pass0[way, half] = y_part(0, way, half, start, count)

    def x_near(half):
        got(near1[0, half], near1[1, half])
        with_sibling(0, 1, half, (yb, yb_row(1, 0)), (yb, yb_row(1, 1)))
        near_x[half] = send(part(p, wrow(0, 1), S, half), part(xb, 0, S, half), other_h)

    def total_of(half):
        got(core[0, 0, half], near_x[half], *(c[way, half] for c in (near0, pass0) for way in WAYS))
        cols = pl.ds(*HALF[half])

        @pl.loop(0, S // 16)
        def _(i):
            total = xb[rows(i * 16, 16), cols].astype(F32)
            for src, start in ((p, wrow(0, 0)), (sib, sib_row(0, 0)), (yb, yb_row(0, 0)),
                               (yb, yb_row(0, 1))):
                total += src[rows(start + i * 16, 16), cols].astype(F32)
            grad_ref[rows(i * 16, 16), cols] = total

    def input_grad(l_of, pair):
        at = rows((l_of * 4 + pair % 4) * 2 * S, 2 * S)
        total = dot(w[at, 0:512], g[:, 0:512], 1, 1) + dot(w[at, 768:1408], g[:, 512:1152], 1, 1)
        ig[at, :] = total.astype(BF)

    core, far_x, near1, near0, far0, pass0, near_x = {}, {}, {}, {}, {}, {}, {}

    def za_row(k, way, step):
        return ((k * 2 + way) * 3 + step) * S

    def z_far(k):
        out = []
        for way in (0, 1):
            start, count = CUTS[k][way]
            src = ig.at[rows(arow(4, k) + start, count)]
            out.append(send(src, zh.at[rows((k * 2 + way) * 80, count)], zdev[way]))
        return out

    def z_pass(k, copies, d):
        out = []
        for way, dz in enumerate((d, 8 - d)):
            got(copies[way])
            if d == 3:
                start, count = CUTS[k][way]
                add_rows(ig, arow(dz, k) + start, count, (0, T), (zh, (k * 2 + way) * 80))
            else:
                add_rows(ig, arow(dz, k), S, (0, T), (za, za_row(k, way, 2 - d)))
            src = ig.at[rows(arow(dz, k), S)]
            out.append(send(src, za.at[rows(za_row(k, way, 3 - d), S)], zdev[way]))
        return out

    @pl.loop(0, 2)
    def _(m):
        hidden_pass(a, w, g, h, 0, m)

    weight_grads((2, 1, 3), 1, 0)
    got(*core_w[1])
    hidden_pass(a, w, g, h, 1, 0)
    x_far(0)
    y_other(0)
    hidden_pass(a, w, g, h, 1, 1)
    far_pair = ((z + 4) % 8) // 2

    @pl.loop(0, 2)
    def _(i):
        input_grad((lo + 1 + i) % 2, far_pair)

    zc = {k: z_far(k) for k in (1, 0)}
    weight_grads((2, 1, 3), 1, 1)
    weight_grads((1, 3, 2), 0, 0)
    x_far(1)
    y_other(1)

    @pl.loop(0, 4)
    def _(i):
        input_grad((lo + 1 + i // 2) % 2, far_pair + 1 + 2 * (i % 2))

    zc[1] = z_pass(1, zc[1], 3)
    y_near(0)
    y_far(0)
    zc[0] = z_pass(0, zc[0], 3)
    weight_grads((1, 3, 2), 0, 1)
    y_near(1)
    for half in (0, 1):
        for k in (1, 0):
            weight_grads((0,), k, half)

    @pl.loop(0, 2)
    def _(i):
        input_grad((lo + 1 + i) % 2, far_pair + 2)

    zc[1] = z_pass(1, zc[1], 2)
    x_near(0)
    y_far(1)
    x_near(1)
    zc[0] = z_pass(0, zc[0], 2)
    y_pass(0)
    zc[1] = z_pass(1, zc[1], 1)
    y_pass(1)
    zc[0] = z_pass(0, zc[0], 1)
    got(*zc[1])
    add_rows(ig, arow(0, 1), S, (0, T), (za, za_row(1, 0, 2)), (za, za_row(1, 1, 2)))
    z_x = send(ig.at[rows(arow(0, 1), S)], xl, other_l)
    total_of(0)

    got(*zc[0], z_x)
    total = ig[rows(arow(0, 0), S), :].astype(F32) + xl[...].astype(F32)
    for way in (0, 1):
        total += za[rows(za_row(0, way, 2), S), :].astype(F32)
    ig_ref[...] = total
    total_of(1)
    drain()


def moments(m, v, grad):
    m_new = 0.9 * m + 0.1 * grad
    v_new = 0.95 * v + 0.05 * grad * grad
    return m_new, v_new, m_new / (jnp.sqrt(v_new) + 1e-8)


def finish(dp_ref, grad_hbm, ig_hbm, mask_hbm, mgu_hbm, vgu_hbm, md_hbm, vd_hbm,
           out_hbm, mgu_new, vgu_new, sgu_new, md_new, vd_new, sd_new,
           grad_ref, ig_ref, mask, out, old, new, in_sem, out_sem):
    firsts = (mgu_hbm.at[0], mgu_hbm.at[1], md_hbm)
    seconds = (vgu_hbm.at[0], vgu_hbm.at[1], vd_hbm)
    loads = [
        pltpu.make_async_copy(mask_hbm, mask, in_sem.at[6]),
        pltpu.make_async_copy(grad_hbm, grad_ref, in_sem.at[7]),
        pltpu.make_async_copy(ig_hbm, ig_ref, in_sem.at[8]),
    ]
    for k in range(3):
        loads.append(pltpu.make_async_copy(firsts[k], old.at[2 * k], in_sem.at[2 * k]))
        loads.append(pltpu.make_async_copy(seconds[k], old.at[2 * k + 1], in_sem.at[2 * k + 1]))
    for load in loads:
        load.start()
    loads[2].wait()
    out[...] = ig_ref[...].astype(BF)
    stores = [pltpu.make_async_copy(out, out_hbm, out_sem.at[9])]
    stores[0].start()
    loads[0].wait()
    loads[1].wait()
    scale = jnp.float32(8192.0) ** -0.5
    keep = jnp.where(keep_of(mask, dp_ref[0]) != 0, scale, 0.0)
    rest = grad_ref[:, 1280:1408]
    lanes = ((0, 768), (256, 1024), (512, 1408))
    results = ((mgu_new.at[0], vgu_new.at[0], sgu_new.at[0]),
               (mgu_new.at[1], vgu_new.at[1], sgu_new.at[1]),
               (md_new, vd_new, sd_new))
    for k in range(3):
        tail = (rest, pltpu.roll(rest, 64, 1), grad_ref[:, 1664:PK])[k][:, : F - MAIN]
        parts = [grad_ref[:, n : n + 256] for n in lanes[k]]
        grad = jnp.concatenate([*parts, tail], 1)
        loads[3 + 2 * k].wait()
        loads[4 + 2 * k].wait()
        new[3 * k], new[3 * k + 1], new[3 * k + 2] = moments(
            old[2 * k], old[2 * k + 1], grad * keep
        )
        for n in range(3):
            store = pltpu.make_async_copy(new.at[3 * k + n], results[k][n], out_sem.at[3 * k + n])
            store.start()
            stores.append(store)
    for store in stores:
        store.wait()


VMEM = pl.BlockSpec(memory_space=pltpu.VMEM)
HBM = pl.BlockSpec(memory_space=pltpu.HBM)
sds = jax.ShapeDtypeStruct


def ffn(tokens, cotangent, mask, wgu, wd):
    return pl.pallas_call(
        body,
        name="ffn_grads",
        out_shape=(sds((S, PK), F32), sds((S, T), F32)),
        in_specs=[HBM] * 5,
        out_specs=(VMEM, VMEM),
        scratch_shapes=[
            pltpu.VMEM(mask.shape, jnp.int32),
            pltpu.VMEM(wgu.shape, BF),
            pltpu.VMEM(wd.shape, BF),
            pltpu.SemaphoreType.DMA((5,)),
            pltpu.VMEM((D, 2 * T), BF),
            pltpu.VMEM((D, PK), BF),
            pltpu.VMEM((D, PK), BF),
            pltpu.VMEM((T, 1152), BF),
            pltpu.VMEM((T, 640), BF),
            pltpu.VMEM((D, T), BF),
            pltpu.VMEM((8 * S, PK), BF),
            pltpu.VMEM((2 * 80, PK), BF),
            pltpu.VMEM((4 * S, PK), BF),
            pltpu.VMEM((S, PK), BF),
            pltpu.VMEM((S, PK), BF),
            pltpu.VMEM((12 * S, T), BF),
            pltpu.VMEM((4 * 80, T), BF),
            pltpu.VMEM((S, T), BF),
            pltpu.SemaphoreType.DMA((COPIES,)),
            pltpu.SemaphoreType.DMA((COPIES,)),
        ],
        compiler_params=pltpu.CompilerParams(
            collective_id=0, has_side_effects=True, vmem_limit_bytes=62 << 20
        ),
    )(tokens, cotangent, mask, wgu, wd)


def on_device(tokens, cotangent, mask, wgu, wd, mgu, vgu, md, vd):
    grad, ig = ffn(tokens.T, cotangent.T, mask, wgu, wd.T)
    dp = lax.axis_index("dp").astype(jnp.int32).reshape(1)
    big, down = sds((2, S, F), F32), sds((S, F), F32)
    out = pl.pallas_call(
        finish,
        name="moments",
        out_shape=(sds((S, T), BF), big, big, big, down, down, down),
        in_specs=[pl.BlockSpec(memory_space=pltpu.SMEM)] + [HBM] * 7,
        out_specs=(HBM,) * 7,
        scratch_shapes=[
            pltpu.VMEM((S, PK), F32),
            pltpu.VMEM((S, T), F32),
            pltpu.VMEM(mask.shape, jnp.int32),
            pltpu.VMEM((S, T), BF),
            pltpu.VMEM((6, S, F), F32),
            pltpu.VMEM((9, S, F), F32),
            pltpu.SemaphoreType.DMA((9,)),
            pltpu.SemaphoreType.DMA((10,)),
        ],
        compiler_params=pltpu.CompilerParams(vmem_limit_bytes=62 << 20),
    )(dp, grad, ig, mask, mgu, vgu, md.T, vd.T)
    return (out[0].T, *out[1:4], *(x.T for x in out[4:]))


def solution(mesh):
    return jax.shard_map(
        on_device,
        mesh=mesh,
        in_specs=(
            P("dp", "tensor"),
            P("dp", "tensor"),
            P(None, "tensor"),
            P(None, "dp", "tensor"),
            P("tensor", "dp"),
            P(None, "dp", "tensor"),
            P(None, "dp", "tensor"),
            P("tensor", "dp"),
            P("tensor", "dp"),
        ),
        out_specs=(
            P("dp", "tensor"),
            P(None, "dp", "tensor"),
            P(None, "dp", "tensor"),
            P(None, "dp", "tensor"),
            P("tensor", "dp"),
            P("tensor", "dp"),
            P("tensor", "dp"),
        ),
        check_vma=False,
    )
```

time: 102 us -> 92.6 us (0.908)
  Pallas kernels: 101 us -> 91.8 us
    pallas_call x1, Pallas kernels: 97.6 us -> 88.1 us  [ffn(): pl.pallas_call(body, name='ffn_grads', out_shape=(sds((S, PK), F32), sds(...]
where the time goes in v3:
time: 92.6 us; the launch traced here: 92.5 us
  Pallas kernels  91.8 us (99%)
    pallas_call x1, Pallas kernels, ffn(): pl.pallas_call(body, name='ffn_grads', out_shape=(sds((S, PK), F32), sds(...  88.1 us
    pallas_call x1, Pallas kernels, on_device(): pl.pallas_call(finish, name='moments', out_shape=(sds((S, T), BF), big, b...  3.76 us

profile of v3, /device:TPU:2, one launch (start us, length us, event | category | flops | bytes accessed | tf_op | source)
XLA Modules:
  0.0 92.5 jit_solution(5653689016231681998)
XLA Ops:
  0.6 88.1 %ffn_grads.1 = (f32[144,1792]{1,0:T(8,128)}, f32[144,512]{1,0:T(8,128)}) custom-call(bf16[144,512]{1,0:T(8,128)(2,1)} %bitcast.13, bf16[144,512]{1,0:T(8,128)(2,1)} %bitcast.14, s32[18,576]{1,0:T(8,128)} %mask_hbm.3, bf16[2,144,576]{2,1,0:T(8,128)(2,1)} %wgu_hbm.1, bf16[144,576]{1,0:T(8,128)(2,1)} %bitcast.12), custom_call_target="tpu_custom_call" | custom-call | tf_op jit(solution)/shard_map/ffn_grads/pallas_call | solution.py:493
  88.7 3.8 %moments.1 = (bf16[144,512]{1,0:T(8,128)(2,1)}, f32[2,144,576]{2,1,0:T(8,128)}, f32[2,144,576]{2,1,0:T(8,128)}, f32[2,144,576]{2,1,0:T(8,128)}, f32[144,576]{1,0...) custom-call(s32[1]{0:T(128)} %bitcast.dp_ref, f32[144,1792]{1,0:T(8,128)} %get-tuple-element.16.grad_hbm, ...), custom_call_target="tpu_custom_call" | custom-call | tf_op jit(solution)/shard_map/moments/pallas_call | solution.py:531

commit v4 on v3

--- a/solution.py
+++ b/solution.py
@@ -20,7 +20,6 @@
 GLANES = ((0, 512), (512, 640))
 HLANES = ((0, 256), (256, 384))
 CUTS = (((0, 80), (80, 64)), ((80, 64), (0, 80)))
-PARTS = ((0, 80), (80, 64))
 WAYS = (0, 1)
 COPIES = 128
 
@@ -71,11 +70,10 @@
 
 
 def hidden_pass(a, w, g, h, half, m):
-    tok = rows(m * 256, 256, 256)
-    cot = rows(T + m * 256, 256, 256)
+    tok, mine = rows(m * 256, 256, 256), rows(m * D, D, D)
     first, (gl, gn), (hl, hn) = HALF[half][0], GLANES[half], HLANES[half]
-    both = dot(a[:, tok], w[:, first : first + gn], 0, 0)
-    hg = dot(a[:, cot], w[:, first + gn : first + gn + hn], 0, 0)
+    both = dot(a[mine, 0:256], w[:, first : first + gn], 0, 0)
+    hg = dot(a[mine, 256:512], w[:, first + gn : first + gn + hn], 0, 0)
     gate_grad, up_grad, hidden = grads_of(both[:, :256], both[:, 256:512], hg[:, :256])
     g[tok, gl : gl + 256] = gate_grad.astype(BF)
     g[tok, gl + 256 : gl + 512] = up_grad.astype(BF)
@@ -107,17 +105,12 @@
     other_h, other_l, sibling = (dp_at(0, 1), tensor), (dp, t_at(0, 1)), (dp_at(0, 0, 1), tensor)
     ydev, zdev = (up_y, down_y), (up_z, down_z)
 
-    own_a = rows((lo * 8 + z) * S, S)
-    loads = [
-        pltpu.make_async_copy(src, dst, in_sem.at[n])
-        for n, (src, dst) in enumerate((
-            (tok_hbm, a.at[own_a, pl.ds(0, T)]),
-            (cot_hbm, a.at[own_a, pl.ds(T, T)]),
-            (mask_hbm, mask_ref),
-            (wgu_hbm, wgu_ref),
-            (wd_hbm, wd_ref),
-        ))
-    ]
+    moves = [(mask_hbm, mask_ref), (wgu_hbm, wgu_ref), (wd_hbm, wd_ref)]
+    for m in (0, 1):
+        own = rows((lo * 8 + z) * S + m * D, S)
+        for n, src in enumerate((tok_hbm, cot_hbm)):
+            moves.append((src.at[:, pl.ds(m * 256, 256)], a.at[own, pl.ds(n * 256, 256)]))
+    loads = [pltpu.make_async_copy(*move, in_sem.at[n]) for n, move in enumerate(moves)]
     for load in loads:
         load.start()
 
@@ -159,7 +152,7 @@
         return ref.at[rows(start, count), pl.ds(*HALF[half])]
 
     def part_of(ref, start, part, dev):
-        return same(ref, start + PARTS[part][0], PARTS[part][1], dev)
+        return same(ref, start + part * D, S, dev)
 
     def to_sibling(dy, k):
         w_c.append(same(w, wrow(dy, k), S, sibling))
@@ -168,9 +161,8 @@
         load.wait()
     pack(w, rows(wrow(0, 0), S), keep_of(mask_ref, dp), wgu_ref[0], wgu_ref[1], wd_ref[...])
     pl.semaphore_wait(barrier, len(partners))
-    core_w = ([], [])
-    a_x = same(a, arow(0, 0), S, other_l)
-    a0, a1, a2, a3, b0, b1 = {}, {}, {}, {}, {}, {}
+    core_w, a_l = ([], []), ([], [])
+    a0, a1, a2, a3, b0, b1, a_x = {}, {}, {}, {}, {}, {}, {}
     w0, w1, v0, v1, w_x = {}, {}, {}, {}, {}
 
     def w_send(start, count, half, dev):
@@ -199,56 +191,68 @@
         got(copies[way, part])
         out[way, part] = part_of(a, arow((8 - d, d)[way], k), part, zdev[way])
 
-    for turn in (0, 1):
-        for way in WAYS:
-            a0[way, turn ^ way] = part_of(a, arow(0, 0), turn ^ way, zdev[way])
-    for half in (0, 1):
-        w_start(w0, 0, half)
-        w_x[half] = w_send(wrow(0, 0), S, half, other_h)
+    def a_start(out, k, part):
+        for way in WAYS:
+            out[way, part] = part_of(a, arow(0, k), part, zdev[way])
+
+    def a_both(copies, out, k, d, part):
+        for way in WAYS:
+            a_next(copies, out, k, d, part, way)
+
+    def a_over(dz, part):
+        a_l[part].append(part_of(a, arow(dz, 0), part, other_l))
+
+    def a_third(part):
+        for way in WAYS:
+            if way == part:
+                a_next(a2, a3, 0, 3, part, way)
+            else:
+                got(a2[way, part])
+            a_over((5, 3)[way], part)
+
+    def a_fourth(part):
+        got(a3[part, part])
+        a_over(4, part)
+
+    for n in (0, 1):
+        a_x[n] = part_of(a, arow(0, 0), n, other_l)
+        a_start(a0, 0, n)
+        w_start(w0, 0, n)
+        w_x[n] = w_send(wrow(0, 0), S, n, other_h)
     for half in (0, 1):
         to_sibling(0, 0, half)
-    for way in WAYS:
-        a_next(a0, a1, 0, 1, way, way)
+    a_both(a0, a1, 0, 1, 0)
     w_next(w0, w1, 0, 0)
-    for way in WAYS:
-        a_next(a0, a1, 0, 1, 1 - way, way)
-    for way in WAYS:
-        a_next(a1, a2, 0, 2, way, way)
+    a_both(a0, a1, 0, 1, 1)
+    a_both(a1, a2, 0, 2, 0)
+    got(a_x[0])
+    a_start(b0, 1, 0)
     w_next(w0, w1, 0, 1)
     got(w_x[0])
     w_start(v0, 1, 0)
     to_sibling(0, 1, 0)
-    for way in WAYS:
-        a_next(a1, a2, 0, 2, 1 - way, way)
-    got(a_x)
-    for turn in (0, 1):
-        for way in WAYS:
-            b0[way, turn] = part_of(a, arow(0, 1), turn, zdev[way])
-    a_l = []
-    for way in WAYS:
-        a_next(a2, a3, 0, 3, way, way)
-        a_l.append(part_of(a, arow((5, 3)[way], 0), way, other_l))
+    a_both(a1, a2, 0, 2, 1)
+    got(a_x[1])
+    a_start(b0, 1, 1)
+    a_third(0)
     got(w_x[1])
     w_start(v0, 1, 1)
     to_sibling(0, 1, 1)
     w_last(w1, 0, 0)
-    for way in WAYS:
-        got(a2[way, 1 - way])
-        a_l.append(part_of(a, arow((5, 3)[way], 0), 1 - way, other_l))
+    a_both(b0, b1, 1, 1, 0)
+    a_third(1)
+    a_fourth(0)
     w_last(w1, 0, 1)
-    for way in WAYS:
-        a_next(b0, b1, 1, 1, 0, way)
-    for way in WAYS:
-        got(a3[way, way])
-        a_l.append(part_of(a, arow(4, 0), way, other_l))
     w_next(v0, v1, 1, 0)
-    for way in WAYS:
-        a_next(b0, b1, 1, 1, 1, way)
+    a_both(b0, b1, 1, 1, 1)
+    a_fourth(1)
     w_next(v0, v1, 1, 1)
     w_last(v1, 1, 0)
-    got(*b1.values())
+    got(b1[0, 0], b1[1, 0], *a_l[0], *core_w[0])
+    hidden_pass(a, w, g, h, 0, 0)
     w_last(v1, 1, 1)
-    got(*a_l, *core_w[0])
+    got(b1[0, 1], b1[1, 1], *a_l[1])
+    hidden_pass(a, w, g, h, 0, 1)
 
     def sib_row(dy, k):
         return (dp_at(dy, k) // 2) * S
@@ -256,12 +260,15 @@
     def yb_row(k, way):
         return (k * 2 + way) * S
 
-    def weight_product(at, half):
+    def weight_product(start, half):
+        at = rows(start, 2 * S)
+        ats = [rows(start + m * D, 2 * S) for m in (0, 1)]
+        toks = (slice(0, 256), slice(256, 512))
         first, (gl, gn), (hl, hn) = HALF[half][0], GLANES[half], HLANES[half]
-        p[at, first : first + gn] = dot(a[at, 0:T], g[:, gl : gl + gn], 1, 0).astype(BF)
-        p[at, first + gn : first + gn + hn] = dot(
-            a[at, T : 2 * T], h[:, hl : hl + hn], 1, 0
-        ).astype(BF)
+        total = sum(dot(a[r, 0:256], g[t, gl : gl + gn], 1, 0) for r, t in zip(ats, toks))
+        p[at, first : first + gn] = total.astype(BF)
+        total = sum(dot(a[r, 256:512], h[t, hl : hl + hn], 1, 0) for r, t in zip(ats, toks))
+        p[at, first + gn : first + gn + hn] = total.astype(BF)
 
     def core_copy(dy, k, half, n):
         return pltpu.make_async_remote_copy(
@@ -281,7 +288,7 @@
         @pl.loop(0, len(dys))
         def _(q):
             dy = dys[0] + step * q + third * (q // 2) + 8
-            weight_product(rows(sib_row(dy, k) * 2, 2 * S), half)
+            weight_product(sib_row(dy, k) * 2, half)
             core_copy(dy, k, half, n0 + q).start()
 
     def with_sibling(dy, k, half, *srcs):
@@ -304,20 +311,20 @@
     def y_near(half):
         for way in WAYS:
             with_sibling((1, 3)[way], 0, half)
-            near0[way, half] = y_part(0, way, half, *CUTS[0][1 - way])
+            near0[way, half] = y_part(0, way, half, *CUTS[half][1 - way])
 
     def y_far(half):
         got(far_x[half])
         with_sibling(2, 0, half, (xq, 0))
         for way in WAYS:
-            start, count = CUTS[0][way]
+            start, count = CUTS[half][way]
             src = part(p, wrow(2, 0) + start, count, half)
             far0[way, half] = send(src, part(ya, way * 80, count, half), ydev[way])
 
     def y_pass(half):
         for way in WAYS:
             got(far0[way, half])
-            start, count = CUTS[0][way]
+            start, count = CUTS[half][way]
             to = wrow((1, 3)[way], 0) + start
             add_rows(p, to, count, HALF[half], (ya, way * 80))
             pass0[way, half] = y_part(0, way, half, start, count)
@@ -370,10 +377,6 @@
             out.append(send(src, za.at[rows(za_row(k, way, 3 - d), S)], zdev[way]))
         return out
 
-    @pl.loop(0, 2)
-    def _(m):
-        hidden_pass(a, w, g, h, 0, m)
-
     weight_grads((2, 1, 3), 1, 0)
     got(*core_w[1])
     hidden_pass(a, w, g, h, 1, 0)
@@ -381,44 +384,47 @@
     y_other(0)
     hidden_pass(a, w, g, h, 1, 1)
     far_pair = ((z + 4) % 8) // 2
-
-    @pl.loop(0, 2)
-    def _(i):
-        input_grad((lo + 1 + i) % 2, far_pair)
-
-    zc = {k: z_far(k) for k in (1, 0)}
+    zc = {}
+
+    def beside(k):
+        @pl.loop(0, 2)
+        def _(i):
+            input_grad(lk[k], far_pair + 1 + 2 * i)
+
+        zc[k] = z_pass(k, zc[k], 3)
+
+    input_grad(lk[1], far_pair)
+    zc[1] = z_far(1)
     weight_grads((2, 1, 3), 1, 1)
-    weight_grads((1, 3, 2), 0, 0)
+    input_grad(lk[0], far_pair)
+    zc[0] = z_far(0)
     x_far(1)
     y_other(1)
-
-    @pl.loop(0, 4)
-    def _(i):
-        input_grad((lo + 1 + i // 2) % 2, far_pair + 1 + 2 * (i % 2))
-
-    zc[1] = z_pass(1, zc[1], 3)
+    beside(1)
+    weight_grads((2, 1, 3), 0, 0)
+    beside(0)
+    y_far(0)
     y_near(0)
-    y_far(0)
-    zc[0] = z_pass(0, zc[0], 3)
-    weight_grads((1, 3, 2), 0, 1)
+    weight_grads((2, 1, 3), 0, 1)
+    for half in (0, 1):
+        weight_grads((0,), 1, half)
+    zc[1] = z_pass(1, zc[1], 2)
+    for half in (0, 1):
+        weight_grads((0,), 0, half)
+    x_near(0)
+    y_far(1)
     y_near(1)
-    for half in (0, 1):
-        for k in (1, 0):
-            weight_grads((0,), k, half)
+    x_near(1)
 
     @pl.loop(0, 2)
     def _(i):
         input_grad((lo + 1 + i) % 2, far_pair + 2)
 
-    zc[1] = z_pass(1, zc[1], 2)
-    x_near(0)
-    y_far(1)
-    x_near(1)
     zc[0] = z_pass(0, zc[0], 2)
     y_pass(0)
     zc[1] = z_pass(1, zc[1], 1)
+    zc[0] = z_pass(0, zc[0], 1)
     y_pass(1)
-    zc[0] = z_pass(0, zc[0], 1)
     got(*zc[1])
     add_rows(ig, arow(0, 1), S, (0, T), (za, za_row(1, 0, 2)), (za, za_row(1, 1, 2)))
     z_x = send(ig.at[rows(arow(0, 1), S)], xl, other_l)
@@ -500,8 +506,8 @@
             pltpu.VMEM(mask.shape, jnp.int32),
             pltpu.VMEM(wgu.shape, BF),
             pltpu.VMEM(wd.shape, BF),
-            pltpu.SemaphoreType.DMA((5,)),
-            pltpu.VMEM((D, 2 * T), BF),
+            pltpu.SemaphoreType.DMA((7,)),
+            pltpu.VMEM((2 * D, T), BF),
             pltpu.VMEM((D, PK), BF),
             pltpu.VMEM((D, PK), BF),
             pltpu.VMEM((T, 1152), BF),

time: 92.6 us -> 91 us (0.983)
  Pallas kernels: 91.8 us -> 90.1 us
    pallas_call x1, Pallas kernels: 88.1 us -> 86.3 us  [ffn(): pl.pallas_call(body, name='ffn_grads', out_shape=(sds((S, PK), F32), sds(...]
where the time goes in v4:
time: 91 us; the launch traced here: 90.9 us
  Pallas kernels  90.1 us (99%)
    pallas_call x1, Pallas kernels, ffn(): pl.pallas_call(body, name='ffn_grads', out_shape=(sds((S, PK), F32), sds(...  86.3 us
    pallas_call x1, Pallas kernels, on_device(): pl.pallas_call(finish, name='moments', out_shape=(sds((S, T), BF), big, b...  3.76 us

profile of v4, /device:TPU:2, one launch (start us, length us, event | category | flops | bytes accessed | tf_op | source)
XLA Modules:
  0.0 90.9 jit_solution(11752885717646206953)
XLA Ops:
  0.6 86.3 %ffn_grads.1 = (f32[144,1792]{1,0:T(8,128)}, f32[144,512]{1,0:T(8,128)}) custom-call(bf16[144,512]{1,0:T(8,128)(2,1)} %bitcast.13, bf16[144,512]{1,0:T(8,128)(2,1)} %bitcast.14, s32[18,576]{1,0:T(8,128)} %mask_hbm.3, bf16[2,144,576]{2,1,0:T(8,128)(2,1)} %wgu_hbm.1, bf16[144,576]{1,0:T(8,128)(2,1)} %bitcast.12), custom_call_target="tpu_custom_call" | custom-call | tf_op jit(solution)/shard_map/ffn_grads/pallas_call | solution.py:499
  86.9 3.8 %moments.1 = (bf16[144,512]{1,0:T(8,128)(2,1)}, f32[2,144,576]{2,1,0:T(8,128)}, f32[2,144,576]{2,1,0:T(8,128)}, f32[2,144,576]{2,1,0:T(8,128)}, f32[144,576]{1,0...) custom-call(s32[1]{0:T(128)} %bitcast.dp_ref, f32[144,1792]{1,0:T(8,128)} %get-tuple-element.16.grad_hbm, ...), custom_call_target="tpu_custom_call" | custom-call | tf_op jit(solution)/shard_map/moments/pallas_call | solution.py:537

commit v5 on v4

--- a/solution.py
+++ b/solution.py
@@ -86,8 +86,8 @@
         h[tok, 512:640] = jnp.where(low, hidden, 0.0).astype(BF)
 
 
-def body(tok_hbm, cot_hbm, mask_hbm, wgu_hbm, wd_hbm, grad_ref, ig_ref,
-         mask_ref, wgu_ref, wd_ref, in_sem, a, w, p, g, h, ig, sib, ya, yb, xb, xq, za, zh, xl, send_sem, recv_sem):
+def body(tok_hbm, cot_hbm, mask_hbm, wgu_hbm, wd_hbm, grad_hbm, ig_hbm,
+         grad_ref, ig_ref, out_sem, mask_ref, wgu_ref, wd_ref, in_sem, a, w, p, g, h, ig, sib, ya, yb, xb, xq, za, zh, xl, send_sem, recv_sem):
     dp, tensor = lax.axis_index("dp"), lax.axis_index("tensor")
     y, hi, c = dp // 4, (dp // 2) % 2, dp % 2
     lo, z = tensor // 8, tensor % 8
@@ -334,6 +334,13 @@
         with_sibling(0, 1, half, (yb, yb_row(1, 0)), (yb, yb_row(1, 1)))
         near_x[half] = send(part(p, wrow(0, 1), S, half), part(xb, 0, S, half), other_h)
 
+    stores = []
+
+    def store(src, dst):
+        copy = pltpu.make_async_copy(src, dst, out_sem.at[len(stores)])
+        copy.start()
+        stores.append(copy)
+
     def total_of(half):
         got(core[0, 0, half], near_x[half], *(c[way, half] for c in (near0, pass0) for way in WAYS))
         cols = pl.ds(*HALF[half])
@@ -345,6 +352,8 @@
                                (yb, yb_row(0, 1))):
                 total += src[rows(start + i * 16, 16), cols].astype(F32)
             grad_ref[rows(i * 16, 16), cols] = total
+
+        store(grad_ref.at[:, cols], grad_hbm.at[:, cols])
 
     def input_grad(l_of, pair):
         at = rows((l_of * 4 + pair % 4) * 2 * S, 2 * S)
@@ -435,8 +444,11 @@
     for way in (0, 1):
         total += za[rows(za_row(0, way, 2), S), :].astype(F32)
     ig_ref[...] = total
+    store(ig_ref, ig_hbm)
     total_of(1)
     drain()
+    for copy in stores:
+        copy.wait()
 
 
 def moments(m, v, grad):
@@ -501,8 +513,11 @@
         name="ffn_grads",
         out_shape=(sds((S, PK), F32), sds((S, T), F32)),
         in_specs=[HBM] * 5,
-        out_specs=(VMEM, VMEM),
+        out_specs=(HBM, HBM),
         scratch_shapes=[
+            pltpu.VMEM((S, PK), F32),
+            pltpu.VMEM((S, T), F32),
+            pltpu.SemaphoreType.DMA((3,)),
             pltpu.VMEM(mask.shape, jnp.int32),
             pltpu.VMEM(wgu.shape, BF),
             pltpu.VMEM(wd.shape, BF),

time: 91 us -> 90.6 us (level)
  no operation moved by 1% of the time
where the time goes in v5:
time: 90.6 us; the launch traced here: 90.5 us
  Pallas kernels  89.7 us (99%)
    pallas_call x1, Pallas kernels, ffn(): pl.pallas_call(body, name='ffn_grads', out_shape=(sds((S, PK), F32), sds(...  85.9 us
    pallas_call x1, Pallas kernels, on_device(): pl.pallas_call(finish, name='moments', out_shape=(sds((S, T), BF), big, b...  3.76 us

profile of v5, /device:TPU:2, one launch (start us, length us, event | category | flops | bytes accessed | tf_op | source)
XLA Modules:
  0.0 90.5 jit_solution(9196247747371216417)
XLA Ops:
  0.6 85.9 %ffn_grads.1 = (f32[144,1792]{1,0:T(8,128)}, f32[144,512]{1,0:T(8,128)}) custom-call(bf16[144,512]{1,0:T(8,128)(2,1)} %bitcast.13, bf16[144,512]{1,0:T(8,128)(2,1)} %bitcast.14, s32[18,576]{1,0:T(8,128)} %mask_hbm.3, bf16[2,144,576]{2,1,0:T(8,128)(2,1)} %wgu_hbm.1, bf16[144,576]{1,0:T(8,128)(2,1)} %bitcast.12), custom_call_target="tpu_custom_call" | custom-call | tf_op jit(solution)/shard_map/ffn_grads/pallas_call | solution.py:511
  86.6 3.8 %moments.1 = (bf16[144,512]{1,0:T(8,128)(2,1)}, f32[2,144,576]{2,1,0:T(8,128)}, f32[2,144,576]{2,1,0:T(8,128)}, f32[2,144,576]{2,1,0:T(8,128)}, f32[144,576]{1,0...) custom-call(s32[1]{0:T(128)} %bitcast.dp_ref, f32[144,1792]{1,0:T(8,128)} %get-tuple-element.16.grad_hbm, ...), custom_call_target="tpu_custom_call" | custom-call | tf_op jit(solution)/shard_map/moments/pallas_call | solution.py:552

commit v6 on v5

--- a/solution.py
+++ b/solution.py
@@ -443,7 +443,7 @@
     total = ig[rows(arow(0, 0), S), :].astype(F32) + xl[...].astype(F32)
     for way in (0, 1):
         total += za[rows(za_row(0, way, 2), S), :].astype(F32)
-    ig_ref[...] = total
+    ig_ref[...] = total.astype(BF)
     store(ig_ref, ig_hbm)
     total_of(1)
     drain()
@@ -459,22 +459,19 @@
 
 def finish(dp_ref, grad_hbm, ig_hbm, mask_hbm, mgu_hbm, vgu_hbm, md_hbm, vd_hbm,
            out_hbm, mgu_new, vgu_new, sgu_new, md_new, vd_new, sd_new,
-           grad_ref, ig_ref, mask, out, old, new, in_sem, out_sem):
+           grad_ref, mask, old, new, in_sem, out_sem):
     firsts = (mgu_hbm.at[0], mgu_hbm.at[1], md_hbm)
     seconds = (vgu_hbm.at[0], vgu_hbm.at[1], vd_hbm)
     loads = [
         pltpu.make_async_copy(mask_hbm, mask, in_sem.at[6]),
         pltpu.make_async_copy(grad_hbm, grad_ref, in_sem.at[7]),
-        pltpu.make_async_copy(ig_hbm, ig_ref, in_sem.at[8]),
     ]
     for k in range(3):
         loads.append(pltpu.make_async_copy(firsts[k], old.at[2 * k], in_sem.at[2 * k]))
         loads.append(pltpu.make_async_copy(seconds[k], old.at[2 * k + 1], in_sem.at[2 * k + 1]))
     for load in loads:
         load.start()
-    loads[2].wait()
-    out[...] = ig_ref[...].astype(BF)
-    stores = [pltpu.make_async_copy(out, out_hbm, out_sem.at[9])]
+    stores = [pltpu.make_async_copy(ig_hbm, out_hbm, out_sem.at[9])]
     stores[0].start()
     loads[0].wait()
     loads[1].wait()
@@ -489,8 +486,8 @@
         tail = (rest, pltpu.roll(rest, 64, 1), grad_ref[:, 1664:PK])[k][:, : F - MAIN]
         parts = [grad_ref[:, n : n + 256] for n in lanes[k]]
         grad = jnp.concatenate([*parts, tail], 1)
+        loads[2 + 2 * k].wait()
         loads[3 + 2 * k].wait()
-        loads[4 + 2 * k].wait()
         new[3 * k], new[3 * k + 1], new[3 * k + 2] = moments(
             old[2 * k], old[2 * k + 1], grad * keep
         )
@@ -511,12 +508,12 @@
     return pl.pallas_call(
         body,
         name="ffn_grads",
-        out_shape=(sds((S, PK), F32), sds((S, T), F32)),
+        out_shape=(sds((S, PK), F32), sds((S, T), BF)),
         in_specs=[HBM] * 5,
         out_specs=(HBM, HBM),
         scratch_shapes=[
             pltpu.VMEM((S, PK), F32),
-            pltpu.VMEM((S, T), F32),
+            pltpu.VMEM((S, T), BF),
             pltpu.SemaphoreType.DMA((3,)),
             pltpu.VMEM(mask.shape, jnp.int32),
             pltpu.VMEM(wgu.shape, BF),
@@ -557,12 +554,10 @@
         out_specs=(HBM,) * 7,
         scratch_shapes=[
             pltpu.VMEM((S, PK), F32),
-            pltpu.VMEM((S, T), F32),
             pltpu.VMEM(mask.shape, jnp.int32),
-            pltpu.VMEM((S, T), BF),
             pltpu.VMEM((6, S, F), F32),
             pltpu.VMEM((9, S, F), F32),
-            pltpu.SemaphoreType.DMA((9,)),
+            pltpu.SemaphoreType.DMA((8,)),
             pltpu.SemaphoreType.DMA((10,)),
         ],
         compiler_params=pltpu.CompilerParams(vmem_limit_bytes=62 << 20),

time: 90.6 us -> 92.6 us (1.022)
  Pallas kernels: 89.7 us -> 91.7 us
    pallas_call x1, Pallas kernels: 3.76 us -> 5.76 us  [on_device(): pl.pallas_call(finish, name='moments', out_shape=(sds((S, T), BF), big, b...]
where the time goes in v6:
time: 92.6 us; the launch traced here: 92.5 us
  Pallas kernels  91.7 us (99%)
    pallas_call x1, Pallas kernels, ffn(): pl.pallas_call(body, name='ffn_grads', out_shape=(sds((S, PK), F32), sds(...  85.9 us
    pallas_call x1, Pallas kernels, on_device(): pl.pallas_call(finish, name='moments', out_shape=(sds((S, T), BF), big, b...  5.76 us

profile of v6, /device:TPU:2, one launch (start us, length us, event | category | flops | bytes accessed | tf_op | source)
XLA Modules:
  0.0 92.5 jit_solution(9420384819866891850)
XLA Ops:
  0.6 85.9 %ffn_grads.1 = (f32[144,1792]{1,0:T(8,128)}, bf16[144,512]{1,0:T(8,128)(2,1)}) custom-call(bf16[144,512]{1,0:T(8,128)(2,1)} %bitcast.13, bf16[144,512]{1,0:T(8,128)(2,1)} %bitcast.14, s32[18,576]{1,0:T(8,128)} %mask_hbm.3, bf16[2,144,576]{2,1,0:T(8,128)(2,1)} %wgu_hbm.1, bf16[144,576]{1,0:T(8,128)(2,1)} %bitcast.12), custom_call_target="tpu_custom_call" | custom-call | tf_op jit(solution)/shard_map/ffn_grads/pallas_call | solution.py:508
  86.6 5.8 %moments.1 = (bf16[144,512]{1,0:T(8,128)(2,1)}, f32[2,144,576]{2,1,0:T(8,128)}, f32[2,144,576]{2,1,0:T(8,128)}, f32[2,144,576]{2,1,0:T(8,128)}, f32[144,576]{1,0...) custom-call(s32[1]{0:T(128)} %bitcast.dp_ref, f32[144,1792]{1,0:T(8,128)} %get-tuple-element.16.grad_hbm, ...), custom_call_target="tpu_custom_call" | custom-call | tf_op jit(solution)/shard_map/moments/pallas_call | solution.py:549
